TPU v7x, 128 devices: a whole 4x4x4 slice. The times are simulated.
128 devices in a mesh: row: 4 (over z_lo, core), col: 32 (over x, z_hi, y).
Axes of the slice: x: 4, y: 4, z: 4 (z_hi: 2, z_lo: 2; z = z_hi * 2 + z_lo), core: 2. Of those that a mesh axis runs over, the one named last changes fastest.
Arguments:
- target_points: float32 [3, 65536], P(None, 'row'), may hold values from 0 to 1.5
- source_points: float32 [3, 65536], P(None, 'col'), may hold values from 0 to 1.5
- target_mass: float32 [65536, 128], P(('row', 'col')), may hold values from 0.1 to 1
- source_mass: float32 [65536, 128], P(('col', 'row')), may hold values from 0.1 to 1
- start_dual: bfloat16 [65536, 128], P(('col', 'row')), may hold values from 0.5 to 2
- tile_row: int32 [6144], P(('row', 'col')), may hold values from 0 to 63, as said below
- tile_column: int32 [6144], P(('row', 'col')), may hold values from 0 to 7, as said below
- tile_count: int32 [128], P(('row', 'col')), may hold values from 4 to 48, as said below
Outputs:
- target_dual: float32 [65536, 128], P(('row', 'col'))
- source_dual: float32 [65536, 128], P(('col', 'row'))
Inputs may be any that keep to these rules, and one draw needn't show every extreme that they name: `tile_row`: each device owns 48 consecutive slots, devices in the order row then col; entries give tile rows within the device's band of 64; slots at or past the device's count are padding. Every tile row and every tile column of the whole kernel has a live tile on some device, and no device lists a tile twice among its live slots. `tile_column`: tile columns within the device's band of 8, for the same slots. `tile_count`: live slots of each device; some device is full.
All inputs are finite; a program needn't handle non-finite values.
Results may differ from a plain program's by a relative error of at most 0.00066.
Values may be sent and summed in bfloat16 or wider, within the bound.
A program may use at most 128 MiB of HBM per device.

v0:
```python
import jax
import jax.numpy as jnp
from jax import lax
from jax.sharding import PartitionSpec as P

TILE = 256
ITERS = 2


KERNEL_SCALE = 0.2


def group_weights(target_band, source_band, row_tiles, col_tiles, live_mask):
    target_block = jax.vmap(lambda i: lax.dynamic_slice_in_dim(target_band, i * TILE, TILE, 1))(
        row_tiles
    )
    source_block = jax.vmap(lambda i: lax.dynamic_slice_in_dim(source_band, i * TILE, TILE, 1))(
        col_tiles
    )
    distance = (target_block[:, 0, :, None] - source_block[:, 0, None, :]) ** 2
    distance = distance + (target_block[:, 1, :, None] - source_block[:, 1, None, :]) ** 2
    distance = distance + (target_block[:, 2, :, None] - source_block[:, 2, None, :]) ** 2
    return (jnp.exp(-distance / KERNEL_SCALE) / TILE * live_mask[:, None, None]).astype(
        jnp.bfloat16
    )


def add_blocks(totals, tile_index, products):
    for member in range(products.shape[0]):
        start_row = tile_index[member] * TILE
        current = lax.dynamic_slice_in_dim(totals, start_row, TILE, 0)
        totals = lax.dynamic_update_slice_in_dim(totals, current + products[member], start_row, 0)
    return totals


def slot_group(tile_row, tile_column, tile_total, group):
    first_slot = group * 4
    row_tiles = lax.dynamic_slice_in_dim(tile_row, first_slot, 4)
    col_tiles = lax.dynamic_slice_in_dim(tile_column, first_slot, 4)
    live_mask = (first_slot + jnp.arange(4, dtype=jnp.int32) < tile_total).astype(jnp.float32)
    return (first_slot, row_tiles, col_tiles, live_mask)


def sweep_rows(target_band, source_band, tile_row, tile_column, tile_total, dual_band):
    groups = (tile_total + 3) // 4
    totals = jnp.zeros((target_band.shape[1], dual_band.shape[1]), jnp.float32)
    kept = jnp.zeros((1,), jnp.bfloat16)

    def advance(group, state_pair):
        totals, kept = state_pair
        first_slot, row_tiles, col_tiles, live_mask = slot_group(
            tile_row, tile_column, tile_total, group
        )
        kernel = group_weights(target_band, source_band, row_tiles, col_tiles, live_mask)
        operand = jax.vmap(lambda c: lax.dynamic_slice_in_dim(dual_band, c * TILE, TILE, 0))(
            col_tiles
        )
        products = jnp.einsum("gij,gjb->gib", kernel, operand, preferred_element_type=jnp.float32)
        totals = add_blocks(totals, row_tiles, products)
        return (totals, kept)

    return lax.fori_loop(0, groups, advance, (totals, kept))


def sweep_columns(target_band, source_band, tile_row, tile_column, tile_total, dual_band):
    groups = (tile_total + 3) // 4
    totals = jnp.zeros((source_band.shape[1], dual_band.shape[1]), jnp.float32)

    def advance(group, totals):
        first_slot, row_tiles, col_tiles, live_mask = slot_group(
            tile_row, tile_column, tile_total, group
        )
        kernel = group_weights(target_band, source_band, row_tiles, col_tiles, live_mask)
        operand = jax.vmap(lambda r: lax.dynamic_slice_in_dim(dual_band, r * TILE, TILE, 0))(
            row_tiles
        )
        products = jnp.einsum("gij,gib->gjb", kernel, operand, preferred_element_type=jnp.float32)
        return add_blocks(totals, col_tiles, products)

    return lax.fori_loop(0, groups, advance, totals)


def local(
    target_points,
    source_points,
    target_mass,
    source_mass,
    start_dual,
    tile_row,
    tile_column,
    tile_count,
):
    tile_total = tile_count[0]
    source_low = start_dual
    target_dual = target_mass
    source_dual = source_mass
    for iteration in range(ITERS):
        source_band = lax.all_gather(source_low, "row", axis=0, tiled=True)
        partial_rows, kept = sweep_rows(
            target_points, source_points, tile_row, tile_column, tile_total, source_band
        )
        summed = lax.psum(partial_rows, "col")
        share_rows = summed.shape[0] // lax.axis_size("col")
        row_sums = lax.dynamic_slice_in_dim(
            summed, lax.axis_index("col") * share_rows, share_rows, 0
        )
        target_dual = target_mass / row_sums
        target_low = target_dual.astype(jnp.bfloat16)
        target_band = lax.all_gather(target_low, "col", axis=0, tiled=True)
        partial_cols = sweep_columns(
            target_points, source_points, tile_row, tile_column, tile_total, target_band
        )
        column_sums = lax.psum_scatter(partial_cols, "row", scatter_dimension=0, tiled=True)
        source_dual = source_mass / column_sums
        source_low = source_dual.astype(jnp.bfloat16)
    return (target_dual, source_dual)


def solution(mesh):
    return jax.shard_map(
        local,
        mesh=mesh,
        in_specs=(
            P(None, "row"),
            P(None, "col"),
            P(("row", "col"), None),
            P(("col", "row"), None),
            P(("col", "row"), None),
            P(("row", "col")),
            P(("row", "col")),
            P(("row", "col")),
        ),
        out_specs=(P(("row", "col"), None), P(("col", "row"), None)),
        check_vma=False,
    )
```

profile of v0, /device:TPU:1, one launch (start us, length us, event | category | flops | bytes accessed | tf_op | source)
XLA Modules:
  0.0 2423.8 jit_solution(10136069527540872570)
XLA Ops:
  7.9 9.2 all_gather.12
  20.7 157.0 %while.67 = (s32[]{:T(128)}, f32[16384,128]{1,0:T(8,128)}, s32[]{:T(128)}, s32[48]{0:T(128)S(1)}, f32[3,16384]{1,0:T(4,128)}, /*index=5*/s32[48]{0:T(128)S(1)}, ...) while((s32[]{:T(128)}, f32[16384,128]{1,0:T(8,128)}, ...), condition=%wide.region_1.2_spmd, body=%wide.region_0.1_spmd.sunk | while | flops 70385720 | bytes 2654346 | solution.py:62
  58.0 8.5 while.82
  89.4 8.5 while.82
  177.7 585.4 %all-reduce.15.cloned.1.call-done = f32[16384,128]{1,0:T(8,128)} async-done(((f32[16384,128]{1,0:T(8,128)}), f32[16384,128]{1,0:T(8,128)}) %all-reduce.15.cloned.1.call-update) | async-done | bytes 8388624 | tf_op jit(solution)/shard_map/psum | solution.py:102
  764.9 100.9 %all-gather.3.cloned.1.call-done = bf16[16384,128]{1,0:T(8,128)(2,1)} async-done(((bf16[512,128]{1,0:T(8,128)(2,1)}), bf16[16384,128]{1,0:T(8,128)(2,1)}) %all-gather.3.cloned.1.call-update) | async-done | bytes 4194320 | tf_op jit(solution)/shard_map/all_gather | solution.py:109
  865.8 136.5 %while.71 = (s32[]{:T(128)}, f32[2048,128]{1,0:T(8,128)S(1)}, s32[]{:T(128)}, s32[48]{0:T(128)S(1)}, s32[48]{0:T(128)S(1)}, /*index=5*/f32[3,16384]{1,0:T(4,128)...) while((s32[]{:T(128)}, f32[2048,128]{1,0:T(8,128)S(1)}, ...), condition=%wide.region_4.5_spmd, body=%wide.region_3.4_spmd.sunk | while | flops 70385720 | bytes 2654338 | solution.py:80
  879.5 8.7 while.83
  906.8 8.7 while.83
  934.1 8.7 while.83
  961.4 8.7 while.83
  988.7 8.7 while.83
  1003.4 209.4 %reduce-scatter.3.cloned.1.call-done = f32[512,128]{1,0:T(8,128)} async-done(((f32[2048,128]{1,0:T(8,128)}), f32[512,128]{1,0:T(8,128)}) %reduce-scatter.3.cloned.1.call-update) | async-done | bytes 262160 | tf_op jit(solution)/shard_map/reduce_scatter | solution.py:113
  1224.7 156.9 %while.75 = (s32[]{:T(128)}, f32[16384,128]{1,0:T(8,128)}, s32[]{:T(128)}, s32[48]{0:T(128)S(1)}, f32[3,16384]{1,0:T(4,128)}, /*index=5*/s32[48]{0:T(128)S(1)}, ...) while((s32[]{:T(128)}, f32[16384,128]{1,0:T(8,128)}, ...), condition=%wide.region_7.8_spmd, body=%wide.region_6.7_spmd.sunk | while | flops 70385720 | bytes 2654338 | solution.py:62
  1262.1 8.5 while.88
  1381.8 583.7 %all-reduce.17.cloned.1.call-done = f32[16384,128]{1,0:T(8,128)} async-done(((f32[16384,128]{1,0:T(8,128)}), f32[16384,128]{1,0:T(8,128)}) %all-reduce.17.cloned.1.call-update) | async-done | bytes 8388624 | tf_op jit(solution)/shard_map/psum | solution.py:102
  1967.2 101.1 %all-gather.5.cloned.1.call-done = bf16[16384,128]{1,0:T(8,128)(2,1)} async-done(((bf16[512,128]{1,0:T(8,128)(2,1)}), bf16[16384,128]{1,0:T(8,128)(2,1)}) %all-gather.5.cloned.1.call-update) | async-done | bytes 4194320 | tf_op jit(solution)/shard_map/all_gather | solution.py:109
  2068.4 136.5 %while.79 = (s32[]{:T(128)}, f32[2048,128]{1,0:T(8,128)S(1)}, s32[]{:T(128)}, s32[48]{0:T(128)S(1)}, s32[48]{0:T(128)S(1)}, /*index=5*/f32[3,16384]{1,0:T(4,128)...) while((s32[]{:T(128)}, f32[2048,128]{1,0:T(8,128)S(1)}, ...), condition=%wide.region_10.11_spmd, body=%wide.region_9.10_spmd.sunk | while | flops 70385720 | bytes 2654338 | solution.py:80
  2082.1 8.7 while.89
  2109.4 8.7 while.89
  2136.7 8.7 while.89
  2164.0 8.7 while.89
  2191.3 8.7 while.89
  2205.9 209.3 %reduce-scatter.5.cloned.1.call-done = f32[512,128]{1,0:T(8,128)} async-done(((f32[2048,128]{1,0:T(8,128)}), f32[512,128]{1,0:T(8,128)}) %reduce-scatter.5.cloned.1.call-update) | async-done | bytes 262160 | tf_op jit(solution)/shard_map/reduce_scatter | solution.py:113
  (1182 shorter events, 861.9 us)
Async XLA Ops:
  7.2 13.5 copy-start.2
  7.2 13.5 copy-start.5
  7.2 13.5 copy-start.6
  7.2 755.9 %all-reduce.15.cloned.1.call-start = ((), (), s32[]{:S(2)}) async-start(), calls=%async_computation.2 | async-start | bytes 16777216 | tf_op jit(solution)/shard_map/psum | solution.py:102
  177.6 585.5 %copy-start.3 = (f32[512,128]{1,0:T(8,128)S(1)}, f32[512,128]{1,0:T(8,128)}, u32[]{:S(2)}) copy-start(f32[512,128]{1,0:T(8,128)} %param.18) | copy-start | bytes 786436
  177.7 688.1 %all-gather.3.cloned.1.call-start = ((), (), s32[]{:S(2)}) async-start(), calls=%async_computation.3 | async-start | bytes 4325376 | tf_op jit(solution)/shard_map/all_gather | solution.py:109
  764.8 448.0 %reduce-scatter.3.cloned.1.call-start = ((), (), s32[]{:S(2)}) async-start(), calls=%async_computation.4 | async-start | bytes 1310720 | tf_op jit(solution)/shard_map/reduce_scatter | solution.py:113
  865.8 347.0 %copy-start.4 = (f32[512,128]{1,0:T(8,128)S(1)}, f32[512,128]{1,0:T(8,128)}, u32[]{:S(2)}) copy-start(f32[512,128]{1,0:T(8,128)} %param.19) | copy-start | bytes 786436
  1002.3 1.0 copy-start
  1003.3 962.1 %all-reduce.17.cloned.1.call-start = ((), (), s32[]{:S(2)}) async-start(), calls=%async_computation.5 | async-start | bytes 16777216 | tf_op jit(solution)/shard_map/psum | solution.py:102
  1381.7 686.6 %all-gather.5.cloned.1.call-start = ((), (), s32[]{:S(2)}) async-start(), calls=%async_computation.6 | async-start | bytes 4325376 | tf_op jit(solution)/shard_map/all_gather | solution.py:109
  1967.2 448.1 %reduce-scatter.5.cloned.1.call-start = ((), (), s32[]{:S(2)}) async-start(), calls=%async_computation.7 | async-start | bytes 1310720 | tf_op jit(solution)/shard_map/reduce_scatter | solution.py:113
  2204.9 1.0 copy-start.1
Sparse Core Ops, SparseCore 0:
  177.8 585.3 all-reduce.14
  766.8 98.9 all-gather.2
  1003.5 209.3 reduce-scatter.2
  1381.8 583.5 all-reduce.16
  1969.4 98.9 all-gather.4
  2206.1 209.1 reduce-scatter.4
where the time goes:
time: 2450 us; the launch traced here: 2420 us
  waiting for transfers between devices  1790 us (73%)
  local copies, waits for them, and re-layouts  442 us (18%)
  other arithmetic  86.4 us (4%)
  loops' own time  55.9 us (2%)
    psum x2, waiting for transfers between devices, local(): summed = lax.psum(partial_rows, 'col')  1170 us
    reduce_scatter x2, waiting for transfers between devices, local(): lax.psum_scatter(partial_cols, 'row', scatter_dimension=0, tiled=True)  419 us
    gather x720, local copies, waits for them, and re-layouts  418 us
    all_gather x2, waiting for transfers between devices, local(): target_band = lax.all_gather(target_low, 'col', axis=0, tiled=True)  202 us
    dynamic_update_slice x80, other arithmetic, add_blocks(): lax.dynamic_update_slice_in_dim(totals, current + products[member], start...  64.1 us
  transfers between devices with their start and end apart: 6, of which 6 were waited for; matrix products, arithmetic and copies ran while one was open for 0% of the time, Pallas kernels for 0%

commit v1 on v0

v1 whole, which is shorter than its diff:
```python
import functools

import jax
import jax.numpy as jnp
from jax import lax
from jax.experimental import pallas as pl
from jax.experimental.pallas import tpu as pltpu
from jax.sharding import PartitionSpec as P

MESH = pl.DeviceIdType.MESH
ITERS = 2
FINE = 2896.0
COARSE = 256.0
F32 = jnp.float32
BF16 = jnp.bfloat16
I16 = jnp.int16
I32 = jnp.int32


def encode(x):
    level = jnp.log(jnp.maximum(x, 1e-37))
    ref = (level[0:1] * COARSE + 32768.5).astype(I32) - 32768
    fine = (level - ref.astype(F32) * (1.0 / COARSE)) * FINE + 32768.5
    code = jnp.clip(fine, 0.5, 65535.0).astype(I32) - 32768
    return code.astype(I16), ref


def decode(code, ref):
    return jnp.exp(
        code.astype(I32).astype(F32) * (1.0 / FINE) + ref.astype(F32) * (1.0 / COARSE)
    )


def kernel(
    slots,
    tp, sp, tm, sm, sd, tr, tc, tn,
    td_out, so_out,
    meta_own, meta_in, meta, tp_in, sp_in, tm_in, tt, sb, kt, acc,
    src_own, s_band, x0_send, x0_recv, r1_send, r1_recv, r2_send, r2_recv, part,
    t_band, z_send, z_recv, td_own,
    p_send, p_recv, s_send, s_recv, x_send, x_recv, a_send, a_recv, b_send, b_recv,
    q_send, q_recv, g_send, g_recv, c_send, c_recv, w_send, w_recv, o_send, o_recv, m_sem,
):
    tile = kt.shape[1]
    measures = acc.shape[1]
    half = measures // 2
    row = lax.axis_index("row")
    col = lax.axis_index("col")
    z_lo, core = row // 2, row % 2
    x, z_hi, y = col // 8, (col // 4) % 2, col % 4
    z = z_hi * 2 + z_lo
    other = 1 - core
    own_role = core == z_hi
    swapped = core != z_hi

    def device(x_, y_, z_, core_):
        return ((z_ % 2) * 2 + core_, x_ * 8 + (z_ // 2) * 4 + y_)

    sibling = device(x, y, z, other)
    partner = device(x, y, core * 2 + z_lo, z_hi)

    def on_ring(axis, step):
        if axis == 0:
            return device((x + step) % 4, y, z, core)
        return device(x, (y + step) % 4, z, core)

    def remote(src, dst, send, recv, target):
        return pltpu.make_async_remote_copy(
            src_ref=src, dst_ref=dst, send_sem=send, recv_sem=recv,
            device_id=target, device_id_type=MESH,
        )

    barrier = pltpu.get_barrier_semaphore()
    friends = [device(x, y, (z + dz) % 4, (core + dk) % 2)
               for dz in range(4) for dk in range(2) if dz or dk]
    friends += [on_ring(axis, step) for axis in (0, 1) for step in (1, 3)]
    for friend in friends:
        pl.semaphore_signal(barrier, inc=1, device_id=friend, device_id_type=MESH)

    meta_own[...] = jnp.zeros_like(meta_own)
    meta_own[0:1, 0:slots] = jnp.clip(tr[...], 0, 63)
    meta_own[1:2, 0:slots] = jnp.clip(tc[...], 0, 7)
    lane = lax.broadcasted_iota(I32, (128, 128), 1)
    sub = lax.broadcasted_iota(I32, (128, 128), 0)
    alive = sub < tn[0]
    for k in range(2):
        across = jnp.broadcast_to(meta_own[k:k + 1, :], (128, 128))
        down = across.T
        same = (down == across) & (sub < lane) & alive
        found = jnp.max(jnp.where(same, sub, -1), axis=0, keepdims=True)
        meta_own[2 + k:3 + k, :] = jnp.where(found < 0, slots, found)
        same = (down == lane) & alive
        found = jnp.max(jnp.where(same, sub, -1), axis=0, keepdims=True)
        meta_own[4 + k:5 + k, :] = jnp.where(found < 0, slots, found)
    index = meta_own[0:1, :]
    share = index // 2
    sx, sh, sy = share // 8, (share // 4) % 2, share % 4
    even = ((sh * 2 + 0) * 4 + sx) * 4 + sy
    odd = ((sh * 2 + 1) * 4 + sy) * 4 + sx
    meta_own[6:7, :] = jnp.where(index % 2 == 0, even, odd)

    pl.semaphore_wait(barrier, len(friends))

    points_out = remote(tp, tp_in, p_send.at[0], p_recv.at[0], sibling)
    sp_copy = remote(sp, sp_in, p_send.at[1], p_recv.at[1], partner)
    meta_copy = remote(meta_own, meta_in, p_send.at[2], p_recv.at[2], partner)
    tm_copy = remote(tm, tm_in, p_send.at[3], p_recv.at[3], partner)

    @pl.when(own_role)
    def _():
        points_out.start()
        sp_in[...] = sp[...]
        tp_in[...] = tp[...]
        tm_in[...] = tm[...]
        meta_in[...] = meta_own[...]

    @pl.when(swapped)
    def _():
        meta_copy.start()
        sp_copy.start()

    def source_copy(it, step):
        return remote(
            src_own.at[it], s_band.at[it, pl.ds(2 * row, 2)],
            s_send.at[step], s_recv.at[it, row], device(x, y, (z + step) % 4, z_hi),
        )

    def source_send(it):
        for step in (1, 2, 3):
            source_copy(it, step).start()

        @pl.when(swapped)
        def _():
            source_copy(it, 0).start()

        @pl.when(own_role)
        def _():
            s_band[it, pl.ds(2 * row, 2)] = src_own[it]

    def source_sent(it):
        for step in (1, 2, 3):
            source_copy(it, step).wait_send()

        @pl.when(swapped)
        def _():
            source_copy(it, 0).wait_send()

    def source_arrived(it):
        for r in range(4):
            @pl.when(jnp.logical_or(swapped, row != r))
            def _():
                remote(src_own.at[it], s_band.at[it, 2 * r:2 * r + 2], s_send.at[0],
                       s_recv.at[it, r], sibling).wait_recv()

    for k in range(2):
        src_own[0, k] = sd[k * tile:(k + 1) * tile, :].astype(F32).T.astype(BF16)
    source_send(0)

    @pl.when(swapped)
    def _():
        tm_copy.start()
        meta_copy.wait_recv()
        sp_copy.wait_recv()
        points_out.wait_recv()

    to_scalar = pltpu.make_async_copy(meta_in, meta, m_sem)
    to_scalar.start()

    @pl.loop(0, 8)
    def _(c):
        start = pl.multiple_of(c * tile, tile)
        for k in range(3):
            line = sp_in[k:k + 1, pl.ds(start, tile)]
            sb[c, k] = jnp.broadcast_to(line, (128, tile)).T

    @pl.loop(0, 64)
    def _(r):
        tt[r, 0:3] = tp_in[:, pl.ds(pl.multiple_of(r * tile, tile), tile)]

    to_scalar.wait()

    @pl.loop(0, slots)
    def _(s):
        r, c = meta[0, s], meta[1, s]
        for part_at in range(tile // 128):
            lanes = slice(part_at * 128, (part_at + 1) * 128)
            distance = (sb[c, 0] - tt[r, 0:1, lanes]) ** 2
            distance = distance + (sb[c, 1] - tt[r, 1:2, lanes]) ** 2
            distance = distance + (sb[c, 2] - tt[r, 2:3, lanes]) ** 2
            weight = jnp.exp(distance * -5.0) * (1.0 / 256.0)
            kt[s, :, part_at * 128:(part_at + 1) * 128] = weight.astype(BF16)

    acc[slots] = jnp.zeros((measures, tile), F32)

    @pl.when(swapped)
    def _():
        tm_copy.wait_recv()

    def total(a, g, u, h):
        gx, gy = (g, u) if a == 0 else (u, g)
        return acc[meta[4, 2 * (gx * 8 + h * 4 + gy) + a]]

    def write_block(ref, n, value):
        rows = value(0).shape[0]
        line = lax.broadcasted_iota(I32, (16, tile), 0)

        def piece(i, refs):
            code, ref_row = encode(value(i))
            ref[pl.ds(pl.multiple_of(i * rows, 16), rows), :] = code
            return jnp.where(line == i, ref_row, refs)

        refs = lax.fori_loop(0, n, piece, jnp.zeros((16, tile), I32))
        ref[n * rows:n * rows + 16, :] = refs.astype(I16)

    def read_block(ref, n, rows, i):
        refs = ref[n * rows:n * rows + 16, :].astype(I32)
        line = lax.broadcasted_iota(I32, (16, tile), 0)
        ref_row = jnp.sum(jnp.where(line == i, refs, 0), axis=0, keepdims=True)
        return decode(ref[pl.ds(pl.multiple_of(i * rows, 16), rows), :], ref_row)

    def iteration(it, _):
        source_arrived(it)

        @pl.loop(0, slots // 2)
        def _(pair):
            products = [
                jnp.dot(s_band[it, meta[1, 2 * pair + m]], kt[2 * pair + m],
                        preferred_element_type=F32)
                for m in range(2)
            ]
            for m in range(2):
                acc[2 * pair + m] = products[m] + acc[meta[2, 2 * pair + m]]

        def x0_copy(a, d):
            return remote(x0_send.at[a, d], x0_recv.at[a, d], x_send.at[a, d],
                          x_recv.at[it, a, d], sibling)

        place = ((x, y), (y, x))
        for d in (2, 1, 3, 0):
            for a in range(2):
                p, _q = place[a]

                @pl.loop(0, 4)
                def _(u):
                    x0_send[a, d, u] = total(a, (p + d) % 4, u, other)

                x0_copy(a, d).start()

        def own(a, d, u):
            return total(a, (place[a][0] + d) % 4, u, core) + x0_recv[a, d, u]

        def r1_copy(a, kind):
            return remote(r1_send.at[a, kind], r1_recv.at[it, a, kind], a_send.at[a, kind],
                          a_recv.at[it, a, kind], on_ring(a, 1 if kind % 2 == 0 else 3))

        for a in range(2):
            x0_copy(a, 2).wait_recv()
            for kind, d, u0 in ((0, 2, 0), (1, 2, 2)):
                write_block(r1_send.at[a, kind], 2, lambda i: own(a, d, u0 + i))
                r1_copy(a, kind).start()
        for a in range(2):
            for kind, d, u0 in ((2, 1, 2), (3, 3, 0)):
                x0_copy(a, d).wait_recv()
                write_block(r1_send.at[a, kind], 2, lambda i: own(a, d, u0 + i))
                r1_copy(a, kind).start()
        for a in range(2):
            for kind, d, u0 in ((4, 1, 0), (5, 3, 2)):
                r1_copy(a, kind - 4).wait_recv()
                got = r1_recv.at[it, a, kind - 4]
                write_block(r1_send.at[a, kind], 2,
                            lambda i: own(a, d, u0 + i) + read_block(got, 2, measures, i))
                r1_copy(a, kind).start()
        for a in range(2):
            x0_copy(a, 0).wait_recv()
            r1_copy(a, 2).wait_recv()
            r1_copy(a, 3).wait_recv()

            @pl.loop(0, 2)
            def _(i):
                part[a, i] = own(a, 0, i) + read_block(r1_recv.at[it, a, 3], 2, measures, i)
                part[a, 2 + i] = own(a, 0, 2 + i) + read_block(
                    r1_recv.at[it, a, 2], 2, measures, i)

            r1_copy(a, 4).wait_recv()
            r1_copy(a, 5).wait_recv()

            @pl.loop(0, 2)
            def _(i):
                part[a, i] += read_block(r1_recv.at[it, a, 4], 2, measures, i)
                part[a, 2 + i] += read_block(r1_recv.at[it, a, 5], 2, measures, i)

        def r2_copy(a, kind):
            return remote(r2_send.at[a, kind], r2_recv.at[it, a, kind], b_send.at[a, kind],
                          b_recv.at[it, a, kind], on_ring(1 - a, 1 if kind % 2 == 0 else 3))

        lower, upper = slice(0, half), slice(half, measures)
        for a in range(2):
            q = place[a][1]
            for kind, d, side in ((0, 2, lower), (1, 2, upper), (2, 1, upper), (3, 3, lower)):
                write_block(r2_send.at[a, kind], 1, lambda i: part[a, (q + d) % 4, side])
                r2_copy(a, kind).start()
        for a in range(2):
            q = place[a][1]
            for kind, d, side in ((4, 1, lower), (5, 3, upper)):
                r2_copy(a, kind - 4).wait_recv()
                got = r2_recv.at[it, a, kind - 4]
                write_block(r2_send.at[a, kind], 1,
                            lambda i: part[a, (q + d) % 4, side] + read_block(got, 1, half, 0))
                r2_copy(a, kind).start()

        def spot(a, g, u):
            return ((core * 2 + a) * 4 + g) * 4 + u

        def q_copy(a, kind):
            p, q = place[a]
            u = (q, q, (q + 3) % 4, (q + 1) % 4)[kind]
            rows = (slice(0, measures), slice(0, measures), lower, upper)[kind]
            ref = t_band.at[it, spot(a, p, u), rows]
            return remote(ref, ref, q_send.at[a, kind], q_recv.at[it, a, kind],
                          on_ring(1 - a, 1 if kind % 2 == 0 else 3))

        def q_got(a, kind):
            p, q = place[a]
            u = ((q + 3) % 4, (q + 1) % 4, (q + 2) % 4, (q + 2) % 4)[kind]
            rows = (slice(0, measures), slice(0, measures), lower, upper)[kind]
            ref = t_band.at[it, spot(a, p, u), rows]
            return remote(ref, ref, q_send.at[a, kind], q_recv.at[it, a, kind], sibling)

        def g_copy(a, du, kind):
            p, q = place[a]
            relay_up = du < 2
            g = p if kind < 2 else ((p + 3) % 4 if relay_up else (p + 1) % 4)
            ref = t_band.at[it, spot(a, g, (q + du) % 4)]
            up = kind == 0 or (kind == 2 and relay_up)
            return remote(ref, ref, g_send.at[a, du, kind], g_recv.at[it, a, du, kind],
                          on_ring(a, 1 if up else 3))

        def g_got(a, du, kind):
            p, q = place[a]
            g = ((p + 3) % 4, (p + 1) % 4, (p + 2) % 4)[kind]
            ref = t_band.at[it, spot(a, g, (q + du) % 4)]
            return remote(ref, ref, g_send.at[a, du, kind], g_recv.at[it, a, du, kind], sibling)

        def c_copy(a, dg):
            ref = t_band.at[it, pl.ds(spot(a, (place[a][0] + dg) % 4, 0), 4)]
            return remote(ref, ref, c_send.at[a, dg], c_recv.at[it, a, dg], sibling)

        def c_got(a, dg):
            base = ((other * 2 + a) * 4 + (place[a][0] + dg) % 4) * 4
            ref = t_band.at[it, pl.ds(base, 4)]
            return remote(ref, ref, c_send.at[a, dg], c_recv.at[it, a, dg], sibling)

        for a in range(2):
            p, q = place[a]
            r2_copy(a, 2).wait_recv()
            r2_copy(a, 3).wait_recv()
            r2_copy(a, 4).wait_recv()
            r2_copy(a, 5).wait_recv()
            got = [read_block(r2_recv.at[it, a, kind], 1, half, 0) for kind in (3, 4, 2, 5)]
            part[a, q, lower] += got[0] + got[1]
            part[a, q, upper] += got[2] + got[3]
            mass = tm_in[a * tile:(a + 1) * tile, :].T
            dual = mass / part[a, q]
            t_band[it, spot(a, p, q)] = dual.astype(BF16)
            q_copy(a, 0).start()
            q_copy(a, 1).start()
            g_copy(a, 0, 0).start()
            g_copy(a, 0, 1).start()

            @pl.when(it == ITERS - 1)
            def _():
                td_own[a * tile:(a + 1) * tile, :] = dual.T

        for a in range(2):
            q_got(a, 0).wait_recv()
            q_copy(a, 2).start()
            g_copy(a, 3, 0).start()
            g_copy(a, 3, 1).start()
            q_got(a, 1).wait_recv()
            q_copy(a, 3).start()
            g_copy(a, 1, 0).start()
            g_copy(a, 1, 1).start()
        for a in range(2):
            g_got(a, 0, 0).wait_recv()
            g_copy(a, 0, 2).start()
            g_got(a, 0, 1).wait_recv()
            q_got(a, 2).wait_recv()
            q_got(a, 3).wait_recv()
            g_copy(a, 2, 0).start()
            g_copy(a, 2, 1).start()
            c_copy(a, 0).start()
        for a in range(2):
            g_got(a, 3, 1).wait_recv()
            g_copy(a, 3, 2).start()
            g_got(a, 1, 0).wait_recv()
            g_copy(a, 1, 2).start()
            g_got(a, 3, 0).wait_recv()
            g_got(a, 1, 1).wait_recv()
            g_got(a, 2, 1).wait_recv()
            g_copy(a, 2, 2).start()
            g_got(a, 2, 0).wait_recv()
            c_copy(a, 3).start()
            c_copy(a, 1).start()
        for a in range(2):
            for du in range(4):
                g_got(a, du, 2).wait_recv()
            c_copy(a, 2).start()
        for dg in (0, 3, 1, 2):
            for a in range(2):
                c_got(a, dg).wait_recv()

        out_copy = remote(td_own, td_out, o_send, o_recv, partner)

        @pl.when(it == ITERS - 1)
        def _():
            @pl.when(swapped)
            def _():
                out_copy.start()

            @pl.when(own_role)
            def _():
                td_out[...] = td_own[...]

        @pl.loop(0, slots // 2)
        def _(pair):
            products = [
                lax.dot_general(t_band[it, meta[6, 2 * pair + m]], kt[2 * pair + m],
                                (((1,), (1,)), ((), ())), preferred_element_type=F32)
                for m in range(2)
            ]
            for m in range(2):
                acc[2 * pair + m] = products[m] + acc[meta[3, 2 * pair + m]]

        def z_copy(r):
            return remote(z_send.at[r], z_recv.at[it, z], w_send.at[r], w_recv.at[it, z],
                          device(x, y, core * 2 + r // 2, r % 2))

        for r in range(4):
            write_block(z_send.at[r], 2, lambda i: acc[meta[5, 2 * r + i]])

            @pl.when(jnp.logical_or(swapped, row != r))
            def _():
                z_copy(r).start()

            @pl.when(jnp.logical_and(own_role, row == r))
            def _():
                z_recv[it, z] = z_send[r]

        for from_z in range(4):
            @pl.when(jnp.logical_or(swapped, z != from_z))
            def _():
                remote(z_send.at[0], z_recv.at[it, from_z], w_send.at[0],
                       w_recv.at[it, from_z], sibling).wait_recv()

        for k in range(2):
            sums = read_block(z_recv.at[it, 0], 2, measures, k)
            for from_z in range(1, 4):
                sums = sums + read_block(z_recv.at[it, from_z], 2, measures, k)
            dual = sm[k * tile:(k + 1) * tile, :].T / sums

            @pl.when(it < ITERS - 1)
            def _():
                src_own[1, k] = dual.astype(BF16)

            @pl.when(it == ITERS - 1)
            def _():
                so_out[k * tile:(k + 1) * tile, :] = dual.T

        source_sent(it)

        @pl.when(it < ITERS - 1)
        def _():
            source_send(1)

        for a in range(2):
            for d in range(4):
                x0_copy(a, d).wait_send()
            for kind in range(6):
                r1_copy(a, kind).wait_send()
                r2_copy(a, kind).wait_send()
            for kind in range(4):
                q_copy(a, kind).wait_send()
            for du in range(4):
                for kind in range(3):
                    g_copy(a, du, kind).wait_send()
                c_copy(a, du).wait_send()
        for r in range(4):
            @pl.when(jnp.logical_or(swapped, row != r))
            def _():
                z_copy(r).wait_send()
        return 0

    lax.fori_loop(0, ITERS, iteration, 0)

    @pl.when(own_role)
    def _():
        points_out.wait_send()

    @pl.when(swapped)
    def _():
        out_copy = remote(td_own, td_out, o_send, o_recv, partner)
        out_copy.wait()
        meta_copy.wait_send()
        sp_copy.wait_send()
        tm_copy.wait_send()


def local(target_points, source_points, target_mass, source_mass, start_dual,
          tile_row, tile_column, tile_count):
    slots = tile_row.shape[0]
    rows, measures = target_mass.shape
    tile = rows // 2
    half = measures // 2
    dma = pltpu.SemaphoreType.DMA
    vmem = pltpu.VMEM
    whole = pl.BlockSpec(memory_space=pltpu.VMEM)
    long_block, short_block = 2 * measures + 16, half + 16
    return pl.pallas_call(
        functools.partial(kernel, slots),
        out_shape=(
            jax.ShapeDtypeStruct((rows, measures), F32),
            jax.ShapeDtypeStruct((rows, measures), F32),
        ),
        in_specs=[whole] * 7 + [pl.BlockSpec(memory_space=pltpu.SMEM)],
        out_specs=(whole, whole),
        scratch_shapes=[
            vmem((8, 128), I32),
            vmem((8, 128), I32),
            pltpu.SMEM((8, 128), I32),
            vmem(target_points.shape, F32),
            vmem(source_points.shape, F32),
            vmem((rows, measures), F32),
            vmem((64, 8, tile), F32),
            vmem((8, 3, tile, 128), F32),
            vmem((slots, tile, tile), BF16),
            vmem((slots + 1, measures, tile), F32),
            vmem((ITERS, 2, measures, tile), BF16),
            vmem((ITERS, 8, measures, tile), BF16),
            vmem((2, 4, 4, measures, tile), F32),
            vmem((2, 4, 4, measures, tile), F32),
            vmem((2, 6, long_block, tile), I16),
            vmem((ITERS, 2, 6, long_block, tile), I16),
            vmem((2, 6, short_block, tile), I16),
            vmem((ITERS, 2, 6, short_block, tile), I16),
            vmem((2, 4, measures, tile), F32),
            vmem((ITERS, 64, measures, tile), BF16),
            vmem((4, long_block, tile), I16),
            vmem((ITERS, 4, long_block, tile), I16),
            vmem((rows, measures), F32),
            dma((4,)), dma((4,)),
            dma((4,)), dma((ITERS, 4)),
            dma((2, 4)), dma((ITERS, 2, 4)),
            dma((2, 6)), dma((ITERS, 2, 6)),
            dma((2, 6)), dma((ITERS, 2, 6)),
            dma((2, 4)), dma((ITERS, 2, 4)),
            dma((2, 4, 3)), dma((ITERS, 2, 4, 3)),
            dma((2, 4)), dma((ITERS, 2, 4)),
            dma((4,)), dma((ITERS, 4)),
            dma, dma, dma,
        ],
        compiler_params=pltpu.CompilerParams(
            collective_id=0, has_side_effects=True, vmem_limit_bytes=60 * 1024 * 1024
        ),
    )(target_points, source_points, target_mass, source_mass, start_dual,
      tile_row.reshape(1, slots), tile_column.reshape(1, slots), tile_count)


def solution(mesh):
    return jax.shard_map(
        local,
        mesh=mesh,
        in_specs=(
            P(None, "row"),
            P(None, "col"),
            P(("row", "col"), None),
            P(("col", "row"), None),
            P(("col", "row"), None),
            P(("row", "col")),
            P(("row", "col")),
            P(("row", "col")),
        ),
        out_specs=(P(("row", "col"), None), P(("col", "row"), None)),
        check_vma=False,
    )
```

time: 2450 us -> 150 us (0.06); the launches traced: 2420 us -> 150 us
  waiting for transfers between devices: 1790 us -> 0 us
  local copies, waits for them, and re-layouts: 442 us -> 2.42 us
  Pallas kernels: 0 us -> 146 us
  other arithmetic: 86.4 us -> 0 us
  loops' own time: 55.9 us -> 0 us
    psum x2 -> x0, waiting for transfers between devices: 1170 us -> none  [local(): summed = lax.psum(partial_rows, 'col')]
    reduce_scatter x2 -> x0, waiting for transfers between devices: 419 us -> none  [local(): lax.psum_scatter(partial_cols, 'row', scatter_dimension=0, tiled=True)]
    gather x720 -> x0, local copies, waits for them, and re-layouts: 418 us -> none
    all_gather x2 -> x0, waiting for transfers between devices: 202 us -> none  [local(): target_band = lax.all_gather(target_low, 'col', axis=0, tiled=True)]
    pallas_call x0 -> x1, Pallas kernels: none -> 146 us  [local(): pl.pallas_call(functools.partial(kernel, slots), out_shape=(jax.ShapeDtyp...]
    dynamic_update_slice x80 -> x0, other arithmetic: 64.1 us -> none  [add_blocks(): lax.dynamic_update_slice_in_dim(totals, current + products[member], start...]
    another operation x64 -> x0, loops' own time: 55.9 us -> none  [the longest x2 27 us: sweep_rows(): return lax.fori_loop(0, groups, advance, (totals, kept))]
  transfers between devices with their start and end apart: 6 -> 0, of which waited for: 6 -> 0; matrix products, arithmetic and copies ran while one was open for 0% -> 0% of each run, Pallas kernels for 0% -> 0%
where the time goes in v1:
time: 150 us
  Pallas kernels  146 us (97%)
  local copies, waits for them, and re-layouts  2.42 us (2%)
    pallas_call x1, Pallas kernels, local(): pl.pallas_call(functools.partial(kernel, slots), out_shape=(jax.ShapeDtyp...  146 us

profile of v1, /device:TPU:1, one launch (start us, length us, event | category | flops | bytes accessed | tf_op | source)
XLA Modules:
  0.0 150.0 jit_solution(2820411520996246571)
XLA Ops:
  1.3 146.2 %shard_map.95 = (f32[512,128]{1,0:T(8,128)}, f32[512,128]{1,0:T(8,128)}) custom-call(f32[3,16384]{1,0:T(4,128)} %tp.1, f32[3,2048]{1,0:T(4,128)} %sp.1, f32[512,128]{1,0:T(8,128)} %tm.1, f32[512,128]{1,0:T(8,128)} %sm.1, bf16[512,128]{1,0:T(8,128)(2,1)} %sd.1, s32[1,48]{1,0:T(1,128)} %bitcast.2, s32[1,48]{1,0:T(1,128)} %bitcast.3, s32[1]{0:T(128)S(6)} %copy.12.tn), custom_call_target="tpu_custom_call" | custom-call | tf_op jit(solution)/shard_map/pallas_call | solution.py:518
  147.5 0.0 copy-start
  147.5 1.7 %copy.13 = f32[512,128]{1,0:T(8,128)} copy(f32[512,128]{1,0:T(8,128)} %get-tuple-element.4) | data formatting | bytes 524288
  149.3 0.0 copy-done
  149.3 0.7 copy.14
Async XLA Ops:
  147.5 1.7 %copy-start = (f32[512,128]{1,0:T(8,128)S(1)}, f32[512,128]{1,0:T(8,128)}, u32[]{:S(2)}) copy-start(f32[512,128]{1,0:T(8,128)} %get-tuple-element.5) | copy-start | bytes 786436

commit v2 on v1

v2 whole, which is shorter than its diff:
```python
import functools

import jax
import jax.numpy as jnp
from jax import lax
from jax.experimental import pallas as pl
from jax.experimental.pallas import tpu as pltpu
from jax.sharding import PartitionSpec as P

MESH = pl.DeviceIdType.MESH
ITERS = 2
CHAINS = 2
LAG = 5.0
GROUP = 4
FINE = 2896.0
COARSE = 256.0
F32 = jnp.float32
BF16 = jnp.bfloat16
I16 = jnp.int16
I32 = jnp.int32


def encode(x):
    level = jnp.log(jnp.maximum(x, 1e-37))
    ref = (level[0:1] * COARSE + 32768.5).astype(I32) - 32768
    fine = (level - ref.astype(F32) * (1.0 / COARSE)) * FINE + 32768.5
    code = jnp.clip(fine, 0.5, 65535.0).astype(I32) - 32768
    return code.astype(I16), ref


def decode(code, ref):
    return jnp.exp(
        code.astype(I32).astype(F32) * (1.0 / FINE) + ref.astype(F32) * (1.0 / COARSE)
    )


def kernel(
    slots,
    tp, sp, tm, sm, sd, tr, tc, tn,
    td_out, so_out,
    meta_own, meta_in, meta, tp_in, sp_in, tm_in, tt, sb, kt, acc,
    src_own, s_band, x0_send, x0_recv, r1_send, r1_recv, r2_send, r2_recv, part,
    t_band, z_send, z_recv, td_own, t_mass, s_mass, t_all, s_all,
    p_send, p_recv, s_send, s_recv, x_send, x_recv, a_send, a_recv, b_send, b_recv,
    q_send, q_recv, g_send, g_recv, c_send, c_recv, w_send, w_recv, o_send, o_recv, m_sem,
):
    tile = kt.shape[1]
    mh = acc.shape[2]
    row = lax.axis_index("row")
    col = lax.axis_index("col")
    z_lo, core = row // 2, row % 2
    x, z_hi, y = col // 8, (col // 4) % 2, col % 4
    z = z_hi * 2 + z_lo
    other = 1 - core
    own_role = core == z_hi
    swapped = core != z_hi

    def device(x_, y_, z_, core_):
        return ((z_ % 2) * 2 + core_, x_ * 8 + (z_ // 2) * 4 + y_)

    sibling = device(x, y, z, other)
    partner = device(x, y, core * 2 + z_lo, z_hi)

    def on_ring(axis, step):
        if axis == 0:
            return device((x + step) % 4, y, z, core)
        return device(x, (y + step) % 4, z, core)

    def remote(src, dst, send, recv, target):
        return pltpu.make_async_remote_copy(
            src_ref=src, dst_ref=dst, send_sem=send, recv_sem=recv,
            device_id=target, device_id_type=MESH,
        )

    barrier = pltpu.get_barrier_semaphore()
    friends = [device(x, y, (z + dz) % 4, (core + dk) % 2)
               for dz in range(4) for dk in range(2) if dz or dk]
    friends += [on_ring(axis, step) for axis in (0, 1) for step in (1, 3)]
    for friend in friends:
        pl.semaphore_signal(barrier, inc=1, device_id=friend, device_id_type=MESH)

    meta_own[...] = jnp.zeros_like(meta_own)
    meta_own[0:1, 0:slots] = jnp.clip(tr[...], 0, 63)
    meta_own[1:2, 0:slots] = jnp.clip(tc[...], 0, 7)
    lane = lax.broadcasted_iota(I32, (128, 128), 1)
    sub = lax.broadcasted_iota(I32, (128, 128), 0)
    alive = sub < tn[0]
    for k in range(2):
        across = jnp.broadcast_to(meta_own[k:k + 1, :], (128, 128))
        down = across.T
        same = (down == across) & (sub < lane) & alive
        found = jnp.max(jnp.where(same, sub, -1), axis=0, keepdims=True)
        meta_own[2 + k:3 + k, :] = jnp.where(found < 0, slots, found)
        same = (down == lane) & alive
        found = jnp.max(jnp.where(same, sub, -1), axis=0, keepdims=True)
        meta_own[4 + k:5 + k, :] = jnp.where(found < 0, slots, found)
    index = meta_own[0:1, :]
    share = index // 2
    sx, sh, sy = share // 8, (share // 4) % 2, share % 4
    even = ((sh * 2 + 0) * 4 + sx) * 4 + sy
    odd = ((sh * 2 + 1) * 4 + sy) * 4 + sx
    meta_own[6:7, :] = jnp.where(index % 2 == 0, even, odd)

    pl.semaphore_wait(barrier, len(friends))

    points_out = remote(tp, tp_in, p_send.at[0], p_recv.at[0], sibling)
    sp_copy = remote(sp, sp_in, p_send.at[1], p_recv.at[1], partner)
    meta_copy = remote(meta_own, meta_in, p_send.at[2], p_recv.at[2], partner)
    tm_copy = remote(tm, tm_in, p_send.at[3], p_recv.at[3], partner)

    @pl.when(own_role)
    def _():
        points_out.start()
        sp_in[...] = sp[...]
        tp_in[...] = tp[...]
        tm_in[...] = tm[...]
        meta_in[...] = meta_own[...]

    @pl.when(swapped)
    def _():
        meta_copy.start()
        sp_copy.start()

    def source_copy(it, h, step):
        return remote(
            src_own.at[it, h], s_band[h].at[it, pl.ds(2 * row, 2)],
            s_send.at[h, step], s_recv.at[it, h, row], device(x, y, (z + step) % 4, z_hi),
        )

    def source_send(it, h):
        for step in (1, 2, 3):
            source_copy(it, h, step).start()

        @pl.when(swapped)
        def _():
            source_copy(it, h, 0).start()

        @pl.when(own_role)
        def _():
            s_band[h][it, pl.ds(2 * row, 2)] = src_own[it, h]

    def source_sent(it, h):
        for step in (1, 2, 3):
            source_copy(it, h, step).wait_send()

        @pl.when(swapped)
        def _():
            source_copy(it, h, 0).wait_send()

    def source_arrived(it, h):
        for r in range(4):
            @pl.when(jnp.logical_or(swapped, row != r))
            def _():
                remote(src_own.at[it, h], s_band[h].at[it, 2 * r:2 * r + 2], s_send.at[h, 0],
                       s_recv.at[it, h, r], sibling).wait_recv()

    for k in range(2):
        start_tile = sd[k * tile:(k + 1) * tile, :].astype(F32).T.astype(BF16)
        for h in range(CHAINS):
            src_own[0, h, k] = start_tile[h * mh:(h + 1) * mh]
    for h in range(CHAINS):
        source_send(0, h)

    @pl.when(swapped)
    def _():
        tm_copy.start()
        meta_copy.wait_recv()
        sp_copy.wait_recv()
        points_out.wait_recv()

    to_scalar = pltpu.make_async_copy(meta_in, meta, m_sem)
    to_scalar.start()

    @pl.loop(0, 8)
    def _(c):
        start = pl.multiple_of(c * tile, tile)
        for k in range(3):
            line = sp_in[k:k + 1, pl.ds(start, tile)]
            sb[c, k] = jnp.broadcast_to(line, (128, tile)).T

    @pl.loop(0, 64)
    def _(r):
        tt[r, 0:3] = tp_in[:, pl.ds(pl.multiple_of(r * tile, tile), tile)]

    to_scalar.wait()

    @pl.loop(0, slots)
    def _(s):
        r, c = meta[0, s], meta[1, s]
        for part_at in range(tile // 128):
            lanes = slice(part_at * 128, (part_at + 1) * 128)
            distance = (sb[c, 0] - tt[r, 0:1, lanes]) ** 2
            distance = distance + (sb[c, 1] - tt[r, 1:2, lanes]) ** 2
            distance = distance + (sb[c, 2] - tt[r, 2:3, lanes]) ** 2
            weight = jnp.exp(distance * -5.0) * (1.0 / 256.0)
            kt[s, :, part_at * 128:(part_at + 1) * 128] = weight.astype(BF16)

    for h in range(CHAINS):
        acc[h, slots] = jnp.zeros((mh, tile), F32)

    @pl.when(swapped)
    def _():
        tm_copy.wait_recv()

    for k in range(2):
        t_mass[k] = tm_in[k * tile:(k + 1) * tile, :].T
        s_mass[k] = sm[k * tile:(k + 1) * tile, :].T

    def write_block(ref, value):
        line = lax.broadcasted_iota(I32, (16, tile), 0)

        def piece(i, refs):
            code, ref_row = encode(value(i))
            ref[pl.ds(pl.multiple_of(i * mh, 16), mh), :] = code
            return jnp.where(line == i, ref_row, refs)

        refs = lax.fori_loop(0, 2, piece, jnp.zeros((16, tile), I32))
        ref[2 * mh:2 * mh + 16, :] = refs.astype(I16)

    def read_block(ref, i):
        refs = ref[2 * mh:2 * mh + 16, :].astype(I32)
        line = lax.broadcasted_iota(I32, (16, tile), 0)
        ref_row = jnp.sum(jnp.where(line == i, refs, 0), axis=0, keepdims=True)
        return decode(ref[pl.ds(pl.multiple_of(i * mh, 16), mh), :], ref_row)

    place = ((x, y), (y, x))
    half = mh // 2
    lower, upper, full = slice(0, half), slice(half, mh), slice(0, mh)
    out_copy = remote(td_own, td_out, o_send, o_recv, partner)

    class Chain:
        def __init__(self, h, it):
            self.h, self.it = h, it

        def x0_copy(self, a, d):
            h = self.h
            return remote(x0_send.at[h, a, d], x0_recv.at[h, a, d], x_send.at[h, a, d],
                          x_recv.at[self.it, h, a, d], sibling)

        def r1_copy(self, a, kind):
            h, it = self.h, self.it
            return remote(r1_send.at[h, a, kind], r1_recv.at[it, h, a, kind],
                          a_send.at[h, a, kind], a_recv.at[it, h, a, kind],
                          on_ring(a, 1 if kind % 2 == 0 else 3))

        def r2_copy(self, a, kind):
            h, it = self.h, self.it
            return remote(r2_send.at[h, a, kind], r2_recv.at[it, h, a, kind],
                          b_send.at[h, a, kind], b_recv.at[it, h, a, kind],
                          on_ring(1 - a, 1 if kind % 2 == 0 else 3))

        def spot(self, a, g, u):
            return ((core * 2 + a) * 4 + g) * 4 + u

        def q_copy(self, a, kind):
            p, q = place[a]
            u = (q, q, (q + 3) % 4, (q + 1) % 4)[kind]
            rows = (full, full, lower, upper)[kind]
            ref = t_band[self.h].at[self.it, self.spot(a, p, u), rows]
            return remote(ref, ref, q_send.at[self.h, a, kind],
                          q_recv.at[self.it, self.h, a, kind],
                          on_ring(1 - a, 1 if kind % 2 == 0 else 3))

        def q_got(self, a, kind):
            p, q = place[a]
            u = ((q + 3) % 4, (q + 1) % 4, (q + 2) % 4, (q + 2) % 4)[kind]
            rows = (full, full, lower, upper)[kind]
            ref = t_band[self.h].at[self.it, self.spot(a, p, u), rows]
            remote(ref, ref, q_send.at[self.h, a, kind],
                   q_recv.at[self.it, self.h, a, kind], sibling).wait_recv()

        def g_copy(self, a, du, kind):
            p, q = place[a]
            relay_up = du < 2
            g = p if kind < 2 else ((p + 3) % 4 if relay_up else (p + 1) % 4)
            ref = t_band[self.h].at[self.it, self.spot(a, g, (q + du) % 4)]
            up = kind == 0 or (kind == 2 and relay_up)
            return remote(ref, ref, g_send.at[self.h, a, du, kind],
                          g_recv.at[self.it, self.h, a, du, kind], on_ring(a, 1 if up else 3))

        def g_got(self, a, du, kind):
            p, q = place[a]
            g = ((p + 3) % 4, (p + 1) % 4, (p + 2) % 4)[kind]
            ref = t_band[self.h].at[self.it, self.spot(a, g, (q + du) % 4)]
            remote(ref, ref, g_send.at[self.h, a, du, kind],
                   g_recv.at[self.it, self.h, a, du, kind], sibling).wait_recv()

        def c_copy(self, a, dg):
            base = self.spot(a, (place[a][0] + dg) % 4, 0)
            ref = t_band[self.h].at[self.it, pl.ds(base, 4)]
            return remote(ref, ref, c_send.at[self.h, a, dg],
                          c_recv.at[self.it, self.h, a, dg], sibling)

        def c_got(self, a, dg):
            base = ((other * 2 + a) * 4 + (place[a][0] + dg) % 4) * 4
            ref = t_band[self.h].at[self.it, pl.ds(base, 4)]
            remote(ref, ref, c_send.at[self.h, a, dg],
                   c_recv.at[self.it, self.h, a, dg], sibling).wait_recv()

        def z_copy(self, r):
            return remote(z_send.at[self.h, r], z_recv.at[self.it, self.h, z],
                          w_send.at[self.h, r], w_recv.at[self.it, self.h, z],
                          device(x, y, core * 2 + r // 2, r % 2))

        def total(self, a, d, u, side):
            g = (place[a][0] + d) % 4
            gx, gy = (g, u) if a == 0 else (u, g)
            return acc[self.h, meta[4, 2 * (gx * 8 + side * 4 + gy) + a]]

        def own(self, a, d, u):
            return self.total(a, d, u, core) + x0_recv[self.h, a, d, u]

        def rows_product(self, begin, end):
            h, it = self.h, self.it

            @pl.loop(begin // GROUP, end // GROUP)
            def _(group):
                at = [group * GROUP + m for m in range(GROUP)]
                products = [jnp.dot(s_band[h][it, meta[1, s]], kt[s],
                                    preferred_element_type=F32) for s in at]
                for s, product in zip(at, products):
                    acc[h, s] = product + acc[h, meta[2, s]]

        def columns_product(self, begin, end):
            h, it = self.h, self.it

            @pl.loop(begin // GROUP, end // GROUP)
            def _(group):
                at = [group * GROUP + m for m in range(GROUP)]
                products = [lax.dot_general(t_band[h][it, meta[6, s]], kt[s],
                                            (((1,), (1,)), ((), ())),
                                            preferred_element_type=F32) for s in at]
                for s, product in zip(at, products):
                    acc[h, s] = product + acc[h, meta[3, s]]

        def rows_first(self):
            source_arrived(self.it, self.h)
            self.rows_product(0, slots // 2)

        def rows_second(self):
            self.rows_product(slots // 2, slots)

        def to_sibling(self):
            for d in (2, 1, 3, 0):
                for a in range(2):
                    @pl.loop(0, 4)
                    def _(u):
                        x0_send[self.h, a, d, u] = self.total(a, d, u, other)

                    self.x0_copy(a, d).start()

        def ring_far(self):
            for a in range(2):
                self.x0_copy(a, 2).wait_recv()
                for kind, d, u0 in ((0, 2, 0), (1, 2, 2)):
                    write_block(r1_send.at[self.h, a, kind], lambda i: self.own(a, d, u0 + i))
                    self.r1_copy(a, kind).start()

        def ring_near(self):
            for a in range(2):
                for kind, d, u0 in ((2, 1, 2), (3, 3, 0)):
                    self.x0_copy(a, d).wait_recv()
                    write_block(r1_send.at[self.h, a, kind], lambda i: self.own(a, d, u0 + i))
                    self.r1_copy(a, kind).start()

        def ring_relay(self):
            for a in range(2):
                for kind, d, u0 in ((4, 1, 0), (5, 3, 2)):
                    self.r1_copy(a, kind - 4).wait_recv()
                    got = r1_recv.at[self.it, self.h, a, kind - 4]
                    write_block(r1_send.at[self.h, a, kind],
                                lambda i: self.own(a, d, u0 + i) + read_block(got, i))
                    self.r1_copy(a, kind).start()

        def ring_sum(self):
            h, it = self.h, self.it
            for a in range(2):
                self.x0_copy(a, 0).wait_recv()
                self.r1_copy(a, 2).wait_recv()
                self.r1_copy(a, 3).wait_recv()

                @pl.loop(0, 2)
                def _(i):
                    part[h, a, i] = self.own(a, 0, i) + read_block(r1_recv.at[it, h, a, 3], i)
                    part[h, a, 2 + i] = self.own(a, 0, 2 + i) + read_block(
                        r1_recv.at[it, h, a, 2], i)

        def ring_total(self):
            h, it = self.h, self.it
            for a in range(2):
                q = place[a][1]
                self.r1_copy(a, 4).wait_recv()
                self.r1_copy(a, 5).wait_recv()

                @pl.loop(0, 2)
                def _(i):
                    part[h, a, i] += read_block(r1_recv.at[it, h, a, 4], i)
                    part[h, a, 2 + i] += read_block(r1_recv.at[it, h, a, 5], i)

                for kind, d, side in ((0, 2, lower), (1, 2, upper), (2, 1, upper), (3, 3, lower)):
                    r2_send[h, a, kind] = part[h, a, (q + d) % 4, side]
                    self.r2_copy(a, kind).start()

        def short_relay(self):
            h, it = self.h, self.it
            for a in range(2):
                q = place[a][1]
                for kind, d, side in ((4, 1, lower), (5, 3, upper)):
                    self.r2_copy(a, kind - 4).wait_recv()
                    r2_send[h, a, kind] = (part[h, a, (q + d) % 4, side]
                                           + r2_recv[it, h, a, kind - 4])
                    self.r2_copy(a, kind).start()

        def target(self):
            h, it = self.h, self.it
            for a in range(2):
                p, q = place[a]
                for kind in (2, 3, 4, 5):
                    self.r2_copy(a, kind).wait_recv()
                sums = part[h, a, q] + jnp.concatenate(
                    [r2_recv[it, h, a, 3] + r2_recv[it, h, a, 4],
                     r2_recv[it, h, a, 2] + r2_recv[it, h, a, 5]], axis=0)
                dual = t_mass[a, h * mh:(h + 1) * mh] / sums
                t_band[h][it, self.spot(a, p, q)] = dual.astype(BF16)
                self.q_copy(a, 0).start()
                self.q_copy(a, 1).start()
                self.g_copy(a, 0, 0).start()
                self.g_copy(a, 0, 1).start()
                t_all[a, h * mh:(h + 1) * mh] = dual

        def gather_near(self):
            for a in range(2):
                self.q_got(a, 0)
                self.q_copy(a, 2).start()
                self.g_copy(a, 3, 0).start()
                self.g_copy(a, 3, 1).start()
                self.q_got(a, 1)
                self.q_copy(a, 3).start()
                self.g_copy(a, 1, 0).start()
                self.g_copy(a, 1, 1).start()

        def gather_far(self):
            for a in range(2):
                self.g_got(a, 0, 0)
                self.g_copy(a, 0, 2).start()
                self.g_got(a, 0, 1)
                self.q_got(a, 2)
                self.q_got(a, 3)
                self.g_copy(a, 2, 0).start()
                self.g_copy(a, 2, 1).start()
                self.c_copy(a, 0).start()

        def gather_relay(self):
            for a in range(2):
                self.g_got(a, 3, 1)
                self.g_copy(a, 3, 2).start()
                self.g_got(a, 1, 0)
                self.g_copy(a, 1, 2).start()
                self.g_got(a, 3, 0)
                self.g_got(a, 1, 1)
                self.g_got(a, 2, 1)
                self.g_copy(a, 2, 2).start()
                self.g_got(a, 2, 0)
                self.c_copy(a, 3).start()
                self.c_copy(a, 1).start()

        def gather_last(self):
            for a in range(2):
                for du in range(4):
                    self.g_got(a, du, 2)
                self.c_copy(a, 2).start()

        def columns_first(self):
            for dg in (0, 3, 1, 2):
                for a in range(2):
                    self.c_got(a, dg)
            self.columns_product(0, slots // 2)

        def columns_second(self):
            self.columns_product(slots // 2, slots)

        def to_owner(self):
            h, it = self.h, self.it
            for r in range(4):
                write_block(z_send.at[h, r], lambda i: acc[h, meta[5, 2 * r + i]])

                @pl.when(jnp.logical_or(swapped, row != r))
                def _():
                    self.z_copy(r).start()

                @pl.when(jnp.logical_and(own_role, row == r))
                def _():
                    z_recv[it, h, z] = z_send[h, r]

        def source(self):
            h, it = self.h, self.it
            for from_z in range(4):
                @pl.when(jnp.logical_or(swapped, z != from_z))
                def _():
                    remote(z_send.at[h, 0], z_recv.at[it, h, from_z], w_send.at[h, 0],
                           w_recv.at[it, h, from_z], sibling).wait_recv()

            for k in range(2):
                sums = read_block(z_recv.at[it, h, 0], k)
                for from_z in range(1, 4):
                    sums = sums + read_block(z_recv.at[it, h, from_z], k)
                dual = s_mass[k, h * mh:(h + 1) * mh] / sums
                s_all[k, h * mh:(h + 1) * mh] = dual

                @pl.when(it < ITERS - 1)
                def _():
                    src_own[1, h, k] = dual.astype(BF16)

            source_sent(it, h)

            @pl.when(it < ITERS - 1)
            def _():
                source_send(1, h)

        def sent(self):
            h = self.h
            for a in range(2):
                for d in range(4):
                    self.x0_copy(a, d).wait_send()
                for kind in range(6):
                    self.r1_copy(a, kind).wait_send()
                    self.r2_copy(a, kind).wait_send()
                for kind in range(4):
                    self.q_copy(a, kind).wait_send()
                for du in range(4):
                    for kind in range(3):
                        self.g_copy(a, du, kind).wait_send()
                    self.c_copy(a, du).wait_send()
            for r in range(4):
                @pl.when(jnp.logical_or(swapped, row != r))
                def _():
                    self.z_copy(r).wait_send()

    moments = (
        (0.0, "rows_first"), (1.7, "rows_second"), (3.4, "to_sibling"), (5.5, "ring_far"),
        (6.2, "ring_near"), (8.3, "ring_relay"), (9.0, "ring_sum"), (11.0, "ring_total"),
        (13.0, "short_relay"), (14.5, "target"), (16.0, "gather_near"), (17.3, "gather_far"),
        (20.0, "gather_relay"), (22.0, "gather_last"), (23.5, "columns_first"),
        (25.0, "columns_second"), (26.7, "to_owner"), (32.0, "source"),
    )
    plan = sorted((moment + LAG * h, h, name) for moment, name in moments for h in range(CHAINS))

    def iteration(it, _):
        chains = [Chain(h, it) for h in range(CHAINS)]
        targets = 0
        for _moment, h, name in plan:
            getattr(chains[h], name)()
            if name == "target":
                targets += 1
                if targets == CHAINS:
                    @pl.when(it == ITERS - 1)
                    def _():
                        for a in range(2):
                            td_own[a * tile:(a + 1) * tile, :] = t_all[a].T

                        @pl.when(swapped)
                        def _():
                            out_copy.start()

                        @pl.when(own_role)
                        def _():
                            td_out[...] = td_own[...]

        for chain in chains:
            chain.sent()
        return 0

    lax.fori_loop(0, ITERS, iteration, 0)
    for k in range(2):
        so_out[k * tile:(k + 1) * tile, :] = s_all[k].T

    @pl.when(own_role)
    def _():
        points_out.wait_send()

    @pl.when(swapped)
    def _():
        out_copy.wait()
        meta_copy.wait_send()
        sp_copy.wait_send()
        tm_copy.wait_send()


def local(target_points, source_points, target_mass, source_mass, start_dual,
          tile_row, tile_column, tile_count):
    slots = tile_row.shape[0]
    rows, measures = target_mass.shape
    tile = rows // 2
    mh = measures // CHAINS
    dma = pltpu.SemaphoreType.DMA
    vmem = pltpu.VMEM
    whole = pl.BlockSpec(memory_space=pltpu.VMEM)
    block = 2 * mh + 16
    return pl.pallas_call(
        functools.partial(kernel, slots),
        out_shape=(
            jax.ShapeDtypeStruct((rows, measures), F32),
            jax.ShapeDtypeStruct((rows, measures), F32),
        ),
        in_specs=[whole] * 7 + [pl.BlockSpec(memory_space=pltpu.SMEM)],
        out_specs=(whole, whole),
        scratch_shapes=[
            vmem((8, 128), I32),
            vmem((8, 128), I32),
            pltpu.SMEM((8, 128), I32),
            vmem(target_points.shape, F32),
            vmem(source_points.shape, F32),
            vmem((rows, measures), F32),
            vmem((64, 8, tile), F32),
            vmem((8, 3, tile, 128), F32),
            vmem((slots, tile, tile), BF16),
            vmem((CHAINS, slots + 1, mh, tile), F32),
            vmem((ITERS, CHAINS, 2, mh, tile), BF16),
            [vmem((ITERS, 8, mh, tile), BF16)] * CHAINS,
            vmem((CHAINS, 2, 4, 4, mh, tile), F32),
            vmem((CHAINS, 2, 4, 4, mh, tile), F32),
            vmem((CHAINS, 2, 6, block, tile), I16),
            vmem((ITERS, CHAINS, 2, 6, block, tile), I16),
            vmem((CHAINS, 2, 6, mh // 2, tile), F32),
            vmem((ITERS, CHAINS, 2, 6, mh // 2, tile), F32),
            vmem((CHAINS, 2, 4, mh, tile), F32),
            [vmem((ITERS, 64, mh, tile), BF16)] * CHAINS,
            vmem((CHAINS, 4, block, tile), I16),
            vmem((ITERS, CHAINS, 4, block, tile), I16),
            vmem((rows, measures), F32),
            vmem((2, measures, tile), F32),
            vmem((2, measures, tile), F32),
            vmem((2, measures, tile), F32),
            vmem((2, measures, tile), F32),
            dma((4,)), dma((4,)),
            dma((CHAINS, 4)), dma((ITERS, CHAINS, 4)),
            dma((CHAINS, 2, 4)), dma((ITERS, CHAINS, 2, 4)),
            dma((CHAINS, 2, 6)), dma((ITERS, CHAINS, 2, 6)),
            dma((CHAINS, 2, 6)), dma((ITERS, CHAINS, 2, 6)),
            dma((CHAINS, 2, 4)), dma((ITERS, CHAINS, 2, 4)),
            dma((CHAINS, 2, 4, 3)), dma((ITERS, CHAINS, 2, 4, 3)),
            dma((CHAINS, 2, 4)), dma((ITERS, CHAINS, 2, 4)),
            dma((CHAINS, 4)), dma((ITERS, CHAINS, 4)),
            dma, dma, dma,
        ],
        compiler_params=pltpu.CompilerParams(
            collective_id=0, has_side_effects=True, vmem_limit_bytes=60 * 1024 * 1024
        ),
    )(target_points, source_points, target_mass, source_mass, start_dual,
      tile_row.reshape(1, slots), tile_column.reshape(1, slots), tile_count)


def solution(mesh):
    return jax.shard_map(
        local,
        mesh=mesh,
        in_specs=(
            P(None, "row"),
            P(None, "col"),
            P(("row", "col"), None),
            P(("col", "row"), None),
            P(("col", "row"), None),
            P(("row", "col")),
            P(("row", "col")),
            P(("row", "col")),
        ),
        out_specs=(P(("row", "col"), None), P(("col", "row"), None)),
        check_vma=False,
    )
```

time: 150 us -> 150 us (level)
  no operation moved by 1% of the time
where the time goes in v2:
time: 150 us; the launch traced here: 149 us
  Pallas kernels  146 us (97%)
  local copies, waits for them, and re-layouts  2.42 us (2%)
    pallas_call x1, Pallas kernels, local(): pl.pallas_call(functools.partial(kernel, slots), out_shape=(jax.ShapeDtyp...  146 us

profile of v2, /device:TPU:1, one launch (start us, length us, event | category | flops | bytes accessed | tf_op | source)
XLA Modules:
  0.0 149.4 jit_solution(2911887712451081522)
XLA Ops:
  1.3 145.7 %shard_map.95 = (f32[512,128]{1,0:T(8,128)}, f32[512,128]{1,0:T(8,128)}) custom-call(f32[3,16384]{1,0:T(4,128)} %tp.1, f32[3,2048]{1,0:T(4,128)} %sp.1, f32[512,128]{1,0:T(8,128)} %tm.1, f32[512,128]{1,0:T(8,128)} %sm.1, bf16[512,128]{1,0:T(8,128)(2,1)} %sd.1, s32[1,48]{1,0:T(1,128)} %bitcast.2, s32[1,48]{1,0:T(1,128)} %bitcast.3, s32[1]{0:T(128)S(6)} %copy.12.tn), custom_call_target="tpu_custom_call" | custom-call | tf_op jit(solution)/shard_map/pallas_call | solution.py:599
  146.9 0.0 copy-start
  147.0 1.7 %copy.13 = f32[512,128]{1,0:T(8,128)} copy(f32[512,128]{1,0:T(8,128)} %get-tuple-element.4) | data formatting | bytes 524288
  148.7 0.0 copy-done
  148.7 0.7 copy.14
Async XLA Ops:
  146.9 1.7 %copy-start = (f32[512,128]{1,0:T(8,128)S(1)}, f32[512,128]{1,0:T(8,128)}, u32[]{:S(2)}) copy-start(f32[512,128]{1,0:T(8,128)} %get-tuple-element.5) | copy-start | bytes 786436

commit v3 on v2

--- a/solution.py
+++ b/solution.py
@@ -9,9 +9,9 @@
 
 MESH = pl.DeviceIdType.MESH
 ITERS = 2
-CHAINS = 2
+CHAINS = 1
 LAG = 5.0
-GROUP = 4
+GROUP = 8
 FINE = 2896.0
 COARSE = 256.0
 F32 = jnp.float32
@@ -61,10 +61,28 @@
     sibling = device(x, y, z, other)
     partner = device(x, y, core * 2 + z_lo, z_hi)
 
+    ring = {(0, step): device((x + step) % 4, y, z, core) for step in (1, 3)}
+    ring.update({(1, step): device(x, (y + step) % 4, z, core) for step in (1, 3)})
+
     def on_ring(axis, step):
-        if axis == 0:
-            return device((x + step) % 4, y, z, core)
-        return device(x, (y + step) % 4, z, core)
+        return ring[axis, step]
+
+    delta = (z + 4 - 2 * core) % 4
+
+    def by_delta(*values):
+        return jnp.where(delta < 2, jnp.where(delta == 0, values[0], values[1]),
+                         jnp.where(delta == 2, values[2], values[3]))
+
+    relayed, single = by_delta(2, 0, 3, 1), by_delta(3, 1, 2, 0)
+    up_band = device(x, y, (z + 1) % 4, z_hi)
+    down_band = device(x, y, (z + 3) % 4, z_hi)
+    up_core = device(x, y, (z + 1) % 4, core)
+    down_core = device(x, y, (z + 3) % 4, core)
+    relay_step = by_delta(3, 1, 1, 3)
+    relay_on = device(x, y, (z + relay_step) % 4, core)
+
+    def owner(r):
+        return device(x, y, core * 2 + r // 2, r % 2)
 
     def remote(src, dst, send, recv, target):
         return pltpu.make_async_remote_copy(
@@ -122,14 +140,19 @@
         sp_copy.start()
 
     def source_copy(it, h, step):
+        target = (sibling, up_band, None, down_band)[step]
         return remote(
             src_own.at[it, h], s_band[h].at[it, pl.ds(2 * row, 2)],
-            s_send.at[h, step], s_recv.at[it, h, row], device(x, y, (z + step) % 4, z_hi),
+            s_send.at[h, step], s_recv.at[it, h, row], target,
         )
 
+    def source_relay(it, h):
+        ref = s_band[h].at[it, pl.ds(2 * relayed, 2)]
+        return remote(ref, ref, s_send.at[h, 2], s_recv.at[it, h, relayed], relay_on)
+
     def source_send(it, h):
-        for step in (1, 2, 3):
-            source_copy(it, h, step).start()
+        source_copy(it, h, 1).start()
+        source_copy(it, h, 3).start()
 
         @pl.when(swapped)
         def _():
@@ -140,16 +163,21 @@
             s_band[h][it, pl.ds(2 * row, 2)] = src_own[it, h]
 
     def source_sent(it, h):
-        for step in (1, 2, 3):
-            source_copy(it, h, step).wait_send()
+        source_copy(it, h, 1).wait_send()
+        source_copy(it, h, 3).wait_send()
+        source_relay(it, h).wait_send()
 
         @pl.when(swapped)
         def _():
             source_copy(it, h, 0).wait_send()
 
+    def source_pass_on(it, h):
+        source_relay(it, h).wait_recv()
+        source_relay(it, h).start()
+
     def source_arrived(it, h):
         for r in range(4):
-            @pl.when(jnp.logical_or(swapped, row != r))
+            @pl.when(jnp.logical_and(jnp.logical_or(swapped, row != r), relayed != r))
             def _():
                 remote(src_own.at[it, h], s_band[h].at[it, 2 * r:2 * r + 2], s_send.at[h, 0],
                        s_recv.at[it, h, r], sibling).wait_recv()
@@ -160,6 +188,9 @@
             src_own[0, h, k] = start_tile[h * mh:(h + 1) * mh]
     for h in range(CHAINS):
         source_send(0, h)
+
+    for h in range(CHAINS):
+        source_pass_on(0, h)
 
     @pl.when(swapped)
     def _():
@@ -297,10 +328,26 @@
             remote(ref, ref, c_send.at[self.h, a, dg],
                    c_recv.at[self.it, self.h, a, dg], sibling).wait_recv()
 
-        def z_copy(self, r):
-            return remote(z_send.at[self.h, r], z_recv.at[self.it, self.h, z],
-                          w_send.at[self.h, r], w_recv.at[self.it, self.h, z],
-                          device(x, y, core * 2 + r // 2, r % 2))
+        def z_copy(self, kind, r):
+            h, it = self.h, self.it
+            return remote(z_send.at[h, r], z_recv.at[it, h, kind], w_send.at[h, r],
+                          w_recv.at[it, h, kind], owner(r))
+
+        def z_far(self, r, target):
+            h, it = self.h, self.it
+            return remote(z_send.at[h, r], z_recv.at[it, h, 3], w_send.at[h, r],
+                          w_recv.at[it, h, 3], target)
+
+        def to_next(self, r, fn):
+            below = (core * 2 + r // 2 + 3) % 4 == z
+
+            @pl.when(below)
+            def _():
+                fn(self.z_copy(1, r))
+
+            @pl.when(jnp.logical_not(below))
+            def _():
+                fn(self.z_copy(2, r))
 
         def total(self, a, d, u, side):
             g = (place[a][0] + d) % 4
@@ -310,35 +357,34 @@
         def own(self, a, d, u):
             return self.total(a, d, u, core) + x0_recv[self.h, a, d, u]
 
-        def rows_product(self, begin, end):
-            h, it = self.h, self.it
+        def products(self, begin, end, one, link):
+            h = self.h
 
             @pl.loop(begin // GROUP, end // GROUP)
             def _(group):
-                at = [group * GROUP + m for m in range(GROUP)]
-                products = [jnp.dot(s_band[h][it, meta[1, s]], kt[s],
-                                    preferred_element_type=F32) for s in at]
-                for s, product in zip(at, products):
-                    acc[h, s] = product + acc[h, meta[2, s]]
+                for m in range(GROUP):
+                    acc[h, group * GROUP + m] = one(group * GROUP + m)
+
+            @pl.loop(begin // 4, end // 4)
+            def _(group):
+                for m in range(4):
+                    s = group * 4 + m
+                    acc[h, s] = acc[h, s] + acc[h, meta[link, s]]
+
+        def rows_product(self, begin, end):
+            h, it = self.h, self.it
+            self.products(begin, end, lambda s: jnp.dot(
+                s_band[h][it, meta[1, s]], kt[s], preferred_element_type=F32), 2)
 
         def columns_product(self, begin, end):
             h, it = self.h, self.it
-
-            @pl.loop(begin // GROUP, end // GROUP)
-            def _(group):
-                at = [group * GROUP + m for m in range(GROUP)]
-                products = [lax.dot_general(t_band[h][it, meta[6, s]], kt[s],
-                                            (((1,), (1,)), ((), ())),
-                                            preferred_element_type=F32) for s in at]
-                for s, product in zip(at, products):
-                    acc[h, s] = product + acc[h, meta[3, s]]
+            self.products(begin, end, lambda s: lax.dot_general(
+                t_band[h][it, meta[6, s]], kt[s], (((1,), (1,)), ((), ())),
+                preferred_element_type=F32), 3)
 
         def rows_first(self):
             source_arrived(self.it, self.h)
-            self.rows_product(0, slots // 2)
-
-        def rows_second(self):
-            self.rows_product(slots // 2, slots)
+            self.rows_product(0, slots)
 
         def to_sibling(self):
             for d in (2, 1, 3, 0):
@@ -474,36 +520,47 @@
             for dg in (0, 3, 1, 2):
                 for a in range(2):
                     self.c_got(a, dg)
-            self.columns_product(0, slots // 2)
-
-        def columns_second(self):
-            self.columns_product(slots // 2, slots)
+            self.columns_product(0, slots)
 
         def to_owner(self):
             h, it = self.h, self.it
-            for r in range(4):
+            first = 2 * (delta % 2)
+            for at in range(2):
+                r = first + at
                 write_block(z_send.at[h, r], lambda i: acc[h, meta[5, 2 * r + i]])
 
-                @pl.when(jnp.logical_or(swapped, row != r))
+                @pl.when(swapped)
                 def _():
-                    self.z_copy(r).start()
-
-                @pl.when(jnp.logical_and(own_role, row == r))
+                    self.z_far(r, device(
+                        x, y, (z + jnp.where((delta == 2) == (at == 0), 3, 1)) % 4, core)).start()
+
+                @pl.when(jnp.logical_and(own_role, core != at))
                 def _():
-                    z_recv[it, h, z] = z_send[h, r]
+                    self.z_copy(0, r).start()
+
+                @pl.when(jnp.logical_and(own_role, core == at))
+                def _():
+                    z_recv[it, h, 0] = z_send[h, r]
+
+            write_block(z_send.at[h, single], lambda i: acc[h, meta[5, 2 * single + i]])
+            self.to_next(single, lambda copy: copy.start())
+            self.z_far(0, sibling).wait_recv()
+            got = z_recv.at[it, h, 3]
+            write_block(z_send.at[h, relayed],
+                        lambda i: acc[h, meta[5, 2 * relayed + i]] + read_block(got, i))
+            self.to_next(relayed, lambda copy: copy.start())
 
         def source(self):
             h, it = self.h, self.it
-            for from_z in range(4):
-                @pl.when(jnp.logical_or(swapped, z != from_z))
+            for kind in range(3):
+                @pl.when(jnp.logical_or(swapped, kind != 0))
                 def _():
-                    remote(z_send.at[h, 0], z_recv.at[it, h, from_z], w_send.at[h, 0],
-                           w_recv.at[it, h, from_z], sibling).wait_recv()
+                    self.z_copy(kind, 0).wait_recv()
 
             for k in range(2):
                 sums = read_block(z_recv.at[it, h, 0], k)
-                for from_z in range(1, 4):
-                    sums = sums + read_block(z_recv.at[it, h, from_z], k)
+                for kind in (1, 2):
+                    sums = sums + read_block(z_recv.at[it, h, kind], k)
                 dual = s_mass[k, h * mh:(h + 1) * mh] / sums
                 s_all[k, h * mh:(h + 1) * mh] = dual
 
@@ -516,6 +573,7 @@
             @pl.when(it < ITERS - 1)
             def _():
                 source_send(1, h)
+                source_pass_on(1, h)
 
         def sent(self):
             h = self.h
@@ -531,17 +589,20 @@
                     for kind in range(3):
                         self.g_copy(a, du, kind).wait_send()
                     self.c_copy(a, du).wait_send()
-            for r in range(4):
-                @pl.when(jnp.logical_or(swapped, row != r))
+            first = 2 * (delta % 2)
+            for at in range(2):
+                @pl.when(jnp.logical_or(swapped, core != at))
                 def _():
-                    self.z_copy(r).wait_send()
+                    self.z_far(first + at, sibling).wait_send()
+            for r in (single, relayed):
+                self.z_copy(1, r).wait_send()
 
     moments = (
-        (0.0, "rows_first"), (1.7, "rows_second"), (3.4, "to_sibling"), (5.5, "ring_far"),
+        (0.0, "rows_first"), (3.4, "to_sibling"), (5.5, "ring_far"),
         (6.2, "ring_near"), (8.3, "ring_relay"), (9.0, "ring_sum"), (11.0, "ring_total"),
         (13.0, "short_relay"), (14.5, "target"), (16.0, "gather_near"), (17.3, "gather_far"),
         (20.0, "gather_relay"), (22.0, "gather_last"), (23.5, "columns_first"),
-        (25.0, "columns_second"), (26.7, "to_owner"), (32.0, "source"),
+        (26.7, "to_owner"), (32.0, "source"),
     )
     plan = sorted((moment + LAG * h, h, name) for moment, name in moments for h in range(CHAINS))
 

time: 150 us -> 146 us (0.973)
  Pallas kernels: 146 us -> 143 us
    pallas_call x1, Pallas kernels: 146 us -> 143 us  [local(): pl.pallas_call(functools.partial(kernel, slots), out_shape=(jax.ShapeDtyp...]
where the time goes in v3:
time: 146 us
  Pallas kernels  143 us (98%)
  local copies, waits for them, and re-layouts  2.42 us (2%)
    pallas_call x1, Pallas kernels, local(): pl.pallas_call(functools.partial(kernel, slots), out_shape=(jax.ShapeDtyp...  143 us

profile of v3, /device:TPU:1, one launch (start us, length us, event | category | flops | bytes accessed | tf_op | source)
XLA Modules:
  0.0 146.3 jit_solution(17220904253198669279)
XLA Ops:
  1.3 142.5 %shard_map.95 = (f32[512,128]{1,0:T(8,128)}, f32[512,128]{1,0:T(8,128)}) custom-call(f32[3,16384]{1,0:T(4,128)} %tp.1, f32[3,2048]{1,0:T(4,128)} %sp.1, f32[512,128]{1,0:T(8,128)} %tm.1, f32[512,128]{1,0:T(8,128)} %sm.1, bf16[512,128]{1,0:T(8,128)(2,1)} %sd.1, s32[1,48]{1,0:T(1,128)} %bitcast.2, s32[1,48]{1,0:T(1,128)} %bitcast.3, s32[1]{0:T(128)S(6)} %copy.12.tn), custom_call_target="tpu_custom_call" | custom-call | tf_op jit(solution)/shard_map/pallas_call | solution.py:660
  143.8 0.0 copy-start
  143.8 1.7 %copy.13 = f32[512,128]{1,0:T(8,128)} copy(f32[512,128]{1,0:T(8,128)} %get-tuple-element.4) | data formatting | bytes 524288
  145.5 0.0 copy-done
  145.6 0.7 copy.14
Async XLA Ops:
  143.8 1.7 %copy-start = (f32[512,128]{1,0:T(8,128)S(1)}, f32[512,128]{1,0:T(8,128)}, u32[]{:S(2)}) copy-start(f32[512,128]{1,0:T(8,128)} %get-tuple-element.5) | copy-start | bytes 786436

commit v4 on v3

--- a/solution.py
+++ b/solution.py
@@ -9,9 +9,9 @@
 
 MESH = pl.DeviceIdType.MESH
 ITERS = 2
-CHAINS = 1
-LAG = 5.0
+CHAINS = 2
 GROUP = 8
+SCALE = 2.6857913
 FINE = 2896.0
 COARSE = 256.0
 F32 = jnp.float32
@@ -45,7 +45,8 @@
     q_send, q_recv, g_send, g_recv, c_send, c_recv, w_send, w_recv, o_send, o_recv, m_sem,
 ):
     tile = kt.shape[1]
-    mh = acc.shape[2]
+    measures = acc.shape[1]
+    mh = measures // CHAINS
     row = lax.axis_index("row")
     col = lax.axis_index("col")
     z_lo, core = row // 2, row % 2
@@ -139,15 +140,18 @@
         meta_copy.start()
         sp_copy.start()
 
+    def rows_of(h):
+        return slice(h * mh, (h + 1) * mh)
+
     def source_copy(it, h, step):
         target = (sibling, up_band, None, down_band)[step]
         return remote(
-            src_own.at[it, h], s_band[h].at[it, pl.ds(2 * row, 2)],
+            src_own.at[it, :, rows_of(h)], s_band.at[it, pl.ds(2 * row, 2), rows_of(h)],
             s_send.at[h, step], s_recv.at[it, h, row], target,
         )
 
     def source_relay(it, h):
-        ref = s_band[h].at[it, pl.ds(2 * relayed, 2)]
+        ref = s_band.at[it, pl.ds(2 * relayed, 2), rows_of(h)]
         return remote(ref, ref, s_send.at[h, 2], s_recv.at[it, h, relayed], relay_on)
 
     def source_send(it, h):
@@ -160,7 +164,7 @@
 
         @pl.when(own_role)
         def _():
-            s_band[h][it, pl.ds(2 * row, 2)] = src_own[it, h]
+            s_band[it, pl.ds(2 * row, 2), rows_of(h)] = src_own[it, :, rows_of(h)]
 
     def source_sent(it, h):
         source_copy(it, h, 1).wait_send()
@@ -179,13 +183,12 @@
         for r in range(4):
             @pl.when(jnp.logical_and(jnp.logical_or(swapped, row != r), relayed != r))
             def _():
-                remote(src_own.at[it, h], s_band[h].at[it, 2 * r:2 * r + 2], s_send.at[h, 0],
+                remote(src_own.at[it, :, rows_of(h)],
+                       s_band.at[it, 2 * r:2 * r + 2, rows_of(h)], s_send.at[h, 0],
                        s_recv.at[it, h, r], sibling).wait_recv()
 
     for k in range(2):
-        start_tile = sd[k * tile:(k + 1) * tile, :].astype(F32).T.astype(BF16)
-        for h in range(CHAINS):
-            src_own[0, h, k] = start_tile[h * mh:(h + 1) * mh]
+        src_own[0, k] = sd[k * tile:(k + 1) * tile, :].astype(F32).T.astype(BF16)
     for h in range(CHAINS):
         source_send(0, h)
 
@@ -206,12 +209,12 @@
     def _(c):
         start = pl.multiple_of(c * tile, tile)
         for k in range(3):
-            line = sp_in[k:k + 1, pl.ds(start, tile)]
+            line = sp_in[k:k + 1, pl.ds(start, tile)] * SCALE
             sb[c, k] = jnp.broadcast_to(line, (128, tile)).T
 
     @pl.loop(0, 64)
     def _(r):
-        tt[r, 0:3] = tp_in[:, pl.ds(pl.multiple_of(r * tile, tile), tile)]
+        tt[r, 0:3] = tp_in[:, pl.ds(pl.multiple_of(r * tile, tile), tile)] * SCALE
 
     to_scalar.wait()
 
@@ -223,11 +226,10 @@
             distance = (sb[c, 0] - tt[r, 0:1, lanes]) ** 2
             distance = distance + (sb[c, 1] - tt[r, 1:2, lanes]) ** 2
             distance = distance + (sb[c, 2] - tt[r, 2:3, lanes]) ** 2
-            weight = jnp.exp(distance * -5.0) * (1.0 / 256.0)
+            weight = jnp.exp2(-8.0 - distance)
             kt[s, :, part_at * 128:(part_at + 1) * 128] = weight.astype(BF16)
 
-    for h in range(CHAINS):
-        acc[h, slots] = jnp.zeros((mh, tile), F32)
+    acc[slots] = jnp.zeros((measures, tile), F32)
 
     @pl.when(swapped)
     def _():
@@ -259,14 +261,26 @@
     lower, upper, full = slice(0, half), slice(half, mh), slice(0, mh)
     out_copy = remote(td_own, td_out, o_send, o_recv, partner)
 
+    def total(a, d, u, side):
+        g = (place[a][0] + d) % 4
+        gx, gy = (g, u) if a == 0 else (u, g)
+        return meta[4, 2 * (gx * 8 + side * 4 + gy) + a]
+
+    def products(one, link):
+        @pl.loop(0, slots // GROUP)
+        def _(group):
+            for m in range(GROUP):
+                s = group * GROUP + m
+                acc[s] = one(s) + acc[meta[link, s]]
+
     class Chain:
         def __init__(self, h, it):
-            self.h, self.it = h, it
-
-        def x0_copy(self, a, d):
+            self.h, self.it, self.rows = h, it, rows_of(h)
+
+        def x0_copy(self, d):
             h = self.h
-            return remote(x0_send.at[h, a, d], x0_recv.at[h, a, d], x_send.at[h, a, d],
-                          x_recv.at[self.it, h, a, d], sibling)
+            return remote(x0_send.at[h, d], x0_recv.at[h, d], x_send.at[h, d],
+                          x_recv.at[self.it, h, d], sibling)
 
         def r1_copy(self, a, kind):
             h, it = self.h, self.it
@@ -280,14 +294,18 @@
                           b_send.at[h, a, kind], b_recv.at[it, h, a, kind],
                           on_ring(1 - a, 1 if kind % 2 == 0 else 3))
 
-        def spot(self, a, g, u):
-            return ((core * 2 + a) * 4 + g) * 4 + u
+        def spot(self, a, g, u, side=None):
+            return (((core if side is None else side) * 2 + a) * 4 + g) * 4 + u
+
+        def some(self, kind):
+            begin = self.h * mh
+            return (self.rows, self.rows, slice(begin, begin + half),
+                    slice(begin + half, begin + mh))[kind]
 
         def q_copy(self, a, kind):
             p, q = place[a]
             u = (q, q, (q + 3) % 4, (q + 1) % 4)[kind]
-            rows = (full, full, lower, upper)[kind]
-            ref = t_band[self.h].at[self.it, self.spot(a, p, u), rows]
+            ref = t_band.at[self.it, self.spot(a, p, u), self.some(kind)]
             return remote(ref, ref, q_send.at[self.h, a, kind],
                           q_recv.at[self.it, self.h, a, kind],
                           on_ring(1 - a, 1 if kind % 2 == 0 else 3))
@@ -295,36 +313,37 @@
         def q_got(self, a, kind):
             p, q = place[a]
             u = ((q + 3) % 4, (q + 1) % 4, (q + 2) % 4, (q + 2) % 4)[kind]
-            rows = (full, full, lower, upper)[kind]
-            ref = t_band[self.h].at[self.it, self.spot(a, p, u), rows]
+            ref = t_band.at[self.it, self.spot(a, p, u), self.some(kind)]
             remote(ref, ref, q_send.at[self.h, a, kind],
                    q_recv.at[self.it, self.h, a, kind], sibling).wait_recv()
 
-        def g_copy(self, a, du, kind):
-            p, q = place[a]
-            relay_up = du < 2
-            g = p if kind < 2 else ((p + 3) % 4 if relay_up else (p + 1) % 4)
-            ref = t_band[self.h].at[self.it, self.spot(a, g, (q + du) % 4)]
-            up = kind == 0 or (kind == 2 and relay_up)
-            return remote(ref, ref, g_send.at[self.h, a, du, kind],
-                          g_recv.at[self.it, self.h, a, du, kind], on_ring(a, 1 if up else 3))
-
-        def g_got(self, a, du, kind):
-            p, q = place[a]
-            g = ((p + 3) % 4, (p + 1) % 4, (p + 2) % 4)[kind]
-            ref = t_band[self.h].at[self.it, self.spot(a, g, (q + du) % 4)]
-            remote(ref, ref, g_send.at[self.h, a, du, kind],
-                   g_recv.at[self.it, self.h, a, du, kind], sibling).wait_recv()
+        def pair(self, a, g, part_at):
+            return t_band.at[self.it, pl.ds(self.spot(a, g, 2 * part_at), 2), self.rows]
+
+        def g_copy(self, a, kind):
+            p = place[a][0]
+            g = (p, p, p, p, (p + 3) % 4, (p + 1) % 4)[kind]
+            ref = self.pair(a, g, (0, 1, 0, 1, 0, 1)[kind])
+            return remote(ref, ref, g_send.at[self.h, a, kind], g_recv.at[self.it, self.h, a, kind],
+                          on_ring(a, (1, 1, 3, 3, 1, 3)[kind]))
+
+        def g_got(self, a, kind):
+            p = place[a][0]
+            g = ((p + 3) % 4, (p + 3) % 4, (p + 1) % 4, (p + 1) % 4,
+                 (p + 2) % 4, (p + 2) % 4)[kind]
+            ref = self.pair(a, g, (0, 1, 0, 1, 0, 1)[kind])
+            remote(ref, ref, g_send.at[self.h, a, kind], g_recv.at[self.it, self.h, a, kind],
+                   sibling).wait_recv()
 
         def c_copy(self, a, dg):
             base = self.spot(a, (place[a][0] + dg) % 4, 0)
-            ref = t_band[self.h].at[self.it, pl.ds(base, 4)]
+            ref = t_band.at[self.it, pl.ds(base, 4), self.rows]
             return remote(ref, ref, c_send.at[self.h, a, dg],
                           c_recv.at[self.it, self.h, a, dg], sibling)
 
         def c_got(self, a, dg):
-            base = ((other * 2 + a) * 4 + (place[a][0] + dg) % 4) * 4
-            ref = t_band[self.h].at[self.it, pl.ds(base, 4)]
+            base = self.spot(a, (place[a][0] + dg) % 4, 0, other)
+            ref = t_band.at[self.it, pl.ds(base, 4), self.rows]
             remote(ref, ref, c_send.at[self.h, a, dg],
                    c_recv.at[self.it, self.h, a, dg], sibling).wait_recv()
 
@@ -349,63 +368,28 @@
             def _():
                 fn(self.z_copy(2, r))
 
-        def total(self, a, d, u, side):
-            g = (place[a][0] + d) % 4
-            gx, gy = (g, u) if a == 0 else (u, g)
-            return acc[self.h, meta[4, 2 * (gx * 8 + side * 4 + gy) + a]]
-
         def own(self, a, d, u):
-            return self.total(a, d, u, core) + x0_recv[self.h, a, d, u]
-
-        def products(self, begin, end, one, link):
-            h = self.h
-
-            @pl.loop(begin // GROUP, end // GROUP)
-            def _(group):
-                for m in range(GROUP):
-                    acc[h, group * GROUP + m] = one(group * GROUP + m)
-
-            @pl.loop(begin // 4, end // 4)
-            def _(group):
-                for m in range(4):
-                    s = group * 4 + m
-                    acc[h, s] = acc[h, s] + acc[h, meta[link, s]]
-
-        def rows_product(self, begin, end):
-            h, it = self.h, self.it
-            self.products(begin, end, lambda s: jnp.dot(
-                s_band[h][it, meta[1, s]], kt[s], preferred_element_type=F32), 2)
-
-        def columns_product(self, begin, end):
-            h, it = self.h, self.it
-            self.products(begin, end, lambda s: lax.dot_general(
-                t_band[h][it, meta[6, s]], kt[s], (((1,), (1,)), ((), ())),
-                preferred_element_type=F32), 3)
-
-        def rows_first(self):
-            source_arrived(self.it, self.h)
-            self.rows_product(0, slots)
-
-        def to_sibling(self):
-            for d in (2, 1, 3, 0):
-                for a in range(2):
-                    @pl.loop(0, 4)
-                    def _(u):
-                        x0_send[self.h, a, d, u] = self.total(a, d, u, other)
-
-                    self.x0_copy(a, d).start()
+            return acc[total(a, d, u, core), self.rows] + x0_recv[self.h, d, a, u]
+
+        def stage(self, d):
+            for a in range(2):
+                @pl.loop(0, 4)
+                def _(u):
+                    x0_send[self.h, d, a, u] = acc[total(a, d, u, other), self.rows]
+
+            self.x0_copy(d).start()
 
         def ring_far(self):
-            for a in range(2):
-                self.x0_copy(a, 2).wait_recv()
+            self.x0_copy(2).wait_recv()
+            for a in range(2):
                 for kind, d, u0 in ((0, 2, 0), (1, 2, 2)):
                     write_block(r1_send.at[self.h, a, kind], lambda i: self.own(a, d, u0 + i))
                     self.r1_copy(a, kind).start()
 
         def ring_near(self):
-            for a in range(2):
-                for kind, d, u0 in ((2, 1, 2), (3, 3, 0)):
-                    self.x0_copy(a, d).wait_recv()
+            for kind, d, u0 in ((2, 1, 2), (3, 3, 0)):
+                self.x0_copy(d).wait_recv()
+                for a in range(2):
                     write_block(r1_send.at[self.h, a, kind], lambda i: self.own(a, d, u0 + i))
                     self.r1_copy(a, kind).start()
 
@@ -420,8 +404,8 @@
 
         def ring_sum(self):
             h, it = self.h, self.it
-            for a in range(2):
-                self.x0_copy(a, 0).wait_recv()
+            self.x0_copy(0).wait_recv()
+            for a in range(2):
                 self.r1_copy(a, 2).wait_recv()
                 self.r1_copy(a, 3).wait_recv()
 
@@ -466,68 +450,57 @@
                 sums = part[h, a, q] + jnp.concatenate(
                     [r2_recv[it, h, a, 3] + r2_recv[it, h, a, 4],
                      r2_recv[it, h, a, 2] + r2_recv[it, h, a, 5]], axis=0)
-                dual = t_mass[a, h * mh:(h + 1) * mh] / sums
-                t_band[h][it, self.spot(a, p, q)] = dual.astype(BF16)
+                dual = t_mass[a, self.rows] / sums
+                t_band[it, self.spot(a, p, q), self.rows] = dual.astype(BF16)
                 self.q_copy(a, 0).start()
                 self.q_copy(a, 1).start()
-                self.g_copy(a, 0, 0).start()
-                self.g_copy(a, 0, 1).start()
-                t_all[a, h * mh:(h + 1) * mh] = dual
+                t_all[a, self.rows] = dual
 
         def gather_near(self):
             for a in range(2):
                 self.q_got(a, 0)
                 self.q_copy(a, 2).start()
-                self.g_copy(a, 3, 0).start()
-                self.g_copy(a, 3, 1).start()
                 self.q_got(a, 1)
                 self.q_copy(a, 3).start()
-                self.g_copy(a, 1, 0).start()
-                self.g_copy(a, 1, 1).start()
-
-        def gather_far(self):
-            for a in range(2):
-                self.g_got(a, 0, 0)
-                self.g_copy(a, 0, 2).start()
-                self.g_got(a, 0, 1)
+
+        def gather_block(self):
+            for a in range(2):
                 self.q_got(a, 2)
                 self.q_got(a, 3)
-                self.g_copy(a, 2, 0).start()
-                self.g_copy(a, 2, 1).start()
+                for kind in (0, 3, 1, 2):
+                    self.g_copy(a, kind).start()
+            for a in range(2):
                 self.c_copy(a, 0).start()
 
         def gather_relay(self):
             for a in range(2):
-                self.g_got(a, 3, 1)
-                self.g_copy(a, 3, 2).start()
-                self.g_got(a, 1, 0)
-                self.g_copy(a, 1, 2).start()
-                self.g_got(a, 3, 0)
-                self.g_got(a, 1, 1)
-                self.g_got(a, 2, 1)
-                self.g_copy(a, 2, 2).start()
-                self.g_got(a, 2, 0)
+                self.g_got(a, 0)
+                self.g_copy(a, 4).start()
+                self.g_got(a, 3)
+                self.g_copy(a, 5).start()
+            for a in range(2):
+                self.g_got(a, 1)
                 self.c_copy(a, 3).start()
+                self.g_got(a, 2)
                 self.c_copy(a, 1).start()
 
         def gather_last(self):
             for a in range(2):
-                for du in range(4):
-                    self.g_got(a, du, 2)
+                self.g_got(a, 4)
+                self.g_got(a, 5)
                 self.c_copy(a, 2).start()
 
-        def columns_first(self):
+        def gathered(self):
             for dg in (0, 3, 1, 2):
                 for a in range(2):
                     self.c_got(a, dg)
-            self.columns_product(0, slots)
 
         def to_owner(self):
             h, it = self.h, self.it
             first = 2 * (delta % 2)
             for at in range(2):
                 r = first + at
-                write_block(z_send.at[h, r], lambda i: acc[h, meta[5, 2 * r + i]])
+                write_block(z_send.at[h, r], lambda i: acc[meta[5, 2 * r + i], self.rows])
 
                 @pl.when(swapped)
                 def _():
@@ -542,12 +515,15 @@
                 def _():
                     z_recv[it, h, 0] = z_send[h, r]
 
-            write_block(z_send.at[h, single], lambda i: acc[h, meta[5, 2 * single + i]])
+            write_block(z_send.at[h, single], lambda i: acc[meta[5, 2 * single + i], self.rows])
             self.to_next(single, lambda copy: copy.start())
+
+        def to_owner_relay(self):
+            h, it = self.h, self.it
             self.z_far(0, sibling).wait_recv()
             got = z_recv.at[it, h, 3]
             write_block(z_send.at[h, relayed],
-                        lambda i: acc[h, meta[5, 2 * relayed + i]] + read_block(got, i))
+                        lambda i: acc[meta[5, 2 * relayed + i], self.rows] + read_block(got, i))
             self.to_next(relayed, lambda copy: copy.start())
 
         def source(self):
@@ -561,34 +537,31 @@
                 sums = read_block(z_recv.at[it, h, 0], k)
                 for kind in (1, 2):
                     sums = sums + read_block(z_recv.at[it, h, kind], k)
-                dual = s_mass[k, h * mh:(h + 1) * mh] / sums
-                s_all[k, h * mh:(h + 1) * mh] = dual
+                dual = s_mass[k, self.rows] / sums
+                s_all[k, self.rows] = dual
 
                 @pl.when(it < ITERS - 1)
                 def _():
-                    src_own[1, h, k] = dual.astype(BF16)
+                    src_own[1, k, self.rows] = dual.astype(BF16)
 
             source_sent(it, h)
 
             @pl.when(it < ITERS - 1)
             def _():
                 source_send(1, h)
-                source_pass_on(1, h)
 
         def sent(self):
             h = self.h
-            for a in range(2):
-                for d in range(4):
-                    self.x0_copy(a, d).wait_send()
+            for d in range(4):
+                self.x0_copy(d).wait_send()
+            for a in range(2):
                 for kind in range(6):
                     self.r1_copy(a, kind).wait_send()
                     self.r2_copy(a, kind).wait_send()
+                    self.g_copy(a, kind).wait_send()
                 for kind in range(4):
                     self.q_copy(a, kind).wait_send()
-                for du in range(4):
-                    for kind in range(3):
-                        self.g_copy(a, du, kind).wait_send()
-                    self.c_copy(a, du).wait_send()
+                    self.c_copy(a, kind).wait_send()
             first = 2 * (delta % 2)
             for at in range(2):
                 @pl.when(jnp.logical_or(swapped, core != at))
@@ -597,35 +570,47 @@
             for r in (single, relayed):
                 self.z_copy(1, r).wait_send()
 
-    moments = (
-        (0.0, "rows_first"), (3.4, "to_sibling"), (5.5, "ring_far"),
-        (6.2, "ring_near"), (8.3, "ring_relay"), (9.0, "ring_sum"), (11.0, "ring_total"),
-        (13.0, "short_relay"), (14.5, "target"), (16.0, "gather_near"), (17.3, "gather_far"),
-        (20.0, "gather_relay"), (22.0, "gather_last"), (23.5, "columns_first"),
-        (26.7, "to_owner"), (32.0, "source"),
-    )
-    plan = sorted((moment + LAG * h, h, name) for moment, name in moments for h in range(CHAINS))
-
     def iteration(it, _):
         chains = [Chain(h, it) for h in range(CHAINS)]
-        targets = 0
-        for _moment, h, name in plan:
-            getattr(chains[h], name)()
-            if name == "target":
-                targets += 1
-                if targets == CHAINS:
-                    @pl.when(it == ITERS - 1)
-                    def _():
-                        for a in range(2):
-                            td_own[a * tile:(a + 1) * tile, :] = t_all[a].T
-
-                        @pl.when(swapped)
-                        def _():
-                            out_copy.start()
-
-                        @pl.when(own_role)
-                        def _():
-                            td_out[...] = td_own[...]
+        for h in range(CHAINS):
+            source_arrived(it, h)
+        products(lambda s: jnp.dot(s_band[it, meta[1, s]], kt[s],
+                                   preferred_element_type=F32), 2)
+        for d in (2, 1, 3, 0):
+            for chain in chains:
+                chain.stage(d)
+        for name in ("ring_far", "ring_near", "ring_relay", "ring_sum", "ring_total",
+                     "short_relay", "target", "gather_near", "gather_block", "gather_relay",
+                     "gather_last"):
+            for chain in chains:
+                getattr(chain, name)()
+
+        @pl.when(it == ITERS - 1)
+        def _():
+            for a in range(2):
+                td_own[a * tile:(a + 1) * tile, :] = t_all[a].T
+
+            @pl.when(swapped)
+            def _():
+                out_copy.start()
+
+            @pl.when(own_role)
+            def _():
+                td_out[...] = td_own[...]
+
+        for chain in chains:
+            chain.gathered()
+        products(lambda s: lax.dot_general(t_band[it, meta[6, s]], kt[s],
+                                           (((1,), (1,)), ((), ())),
+                                           preferred_element_type=F32), 3)
+        for name in ("to_owner", "to_owner_relay", "source"):
+            for chain in chains:
+                getattr(chain, name)()
+
+        @pl.when(it < ITERS - 1)
+        def _():
+            for h in range(CHAINS):
+                source_pass_on(1, h)
 
         for chain in chains:
             chain.sent()
@@ -675,17 +660,17 @@
             vmem((64, 8, tile), F32),
             vmem((8, 3, tile, 128), F32),
             vmem((slots, tile, tile), BF16),
-            vmem((CHAINS, slots + 1, mh, tile), F32),
-            vmem((ITERS, CHAINS, 2, mh, tile), BF16),
-            [vmem((ITERS, 8, mh, tile), BF16)] * CHAINS,
-            vmem((CHAINS, 2, 4, 4, mh, tile), F32),
-            vmem((CHAINS, 2, 4, 4, mh, tile), F32),
+            vmem((slots + 1, measures, tile), F32),
+            vmem((ITERS, 2, measures, tile), BF16),
+            vmem((ITERS, 8, measures, tile), BF16),
+            vmem((CHAINS, 4, 2, 4, mh, tile), F32),
+            vmem((CHAINS, 4, 2, 4, mh, tile), F32),
             vmem((CHAINS, 2, 6, block, tile), I16),
             vmem((ITERS, CHAINS, 2, 6, block, tile), I16),
             vmem((CHAINS, 2, 6, mh // 2, tile), F32),
             vmem((ITERS, CHAINS, 2, 6, mh // 2, tile), F32),
             vmem((CHAINS, 2, 4, mh, tile), F32),
-            [vmem((ITERS, 64, mh, tile), BF16)] * CHAINS,
+            vmem((ITERS, 64, measures, tile), BF16),
             vmem((CHAINS, 4, block, tile), I16),
             vmem((ITERS, CHAINS, 4, block, tile), I16),
             vmem((rows, measures), F32),
@@ -695,11 +680,11 @@
             vmem((2, measures, tile), F32),
             dma((4,)), dma((4,)),
             dma((CHAINS, 4)), dma((ITERS, CHAINS, 4)),
-            dma((CHAINS, 2, 4)), dma((ITERS, CHAINS, 2, 4)),
+            dma((CHAINS, 4)), dma((ITERS, CHAINS, 4)),
             dma((CHAINS, 2, 6)), dma((ITERS, CHAINS, 2, 6)),
             dma((CHAINS, 2, 6)), dma((ITERS, CHAINS, 2, 6)),
             dma((CHAINS, 2, 4)), dma((ITERS, CHAINS, 2, 4)),
-            dma((CHAINS, 2, 4, 3)), dma((ITERS, CHAINS, 2, 4, 3)),
+            dma((CHAINS, 2, 6)), dma((ITERS, CHAINS, 2, 6)),
             dma((CHAINS, 2, 4)), dma((ITERS, CHAINS, 2, 4)),
             dma((CHAINS, 4)), dma((ITERS, CHAINS, 4)),
             dma, dma, dma,

time: 146 us -> 139 us (0.952)
  Pallas kernels: 143 us -> 135 us
    pallas_call x1, Pallas kernels: 143 us -> 135 us  [local(): pl.pallas_call(functools.partial(kernel, slots), out_shape=(jax.ShapeDtyp...]
where the time goes in v4:
time: 139 us
  Pallas kernels  135 us (97%)
  local copies, waits for them, and re-layouts  2.42 us (2%)
    pallas_call x1, Pallas kernels, local(): pl.pallas_call(functools.partial(kernel, slots), out_shape=(jax.ShapeDtyp...  135 us

profile of v4, /device:TPU:1, one launch (start us, length us, event | category | flops | bytes accessed | tf_op | source)
XLA Modules:
  0.0 139.0 jit_solution(1285751871933541180)
XLA Ops:
  1.3 135.3 %shard_map.95 = (f32[512,128]{1,0:T(8,128)}, f32[512,128]{1,0:T(8,128)}) custom-call(f32[3,16384]{1,0:T(4,128)} %tp.1, f32[3,2048]{1,0:T(4,128)} %sp.1, f32[512,128]{1,0:T(8,128)} %tm.1, f32[512,128]{1,0:T(8,128)} %sm.1, bf16[512,128]{1,0:T(8,128)(2,1)} %sd.1, s32[1,48]{1,0:T(1,128)} %bitcast.2, s32[1,48]{1,0:T(1,128)} %bitcast.3, s32[1]{0:T(128)S(6)} %copy.12.tn), custom_call_target="tpu_custom_call" | custom-call | tf_op jit(solution)/shard_map/pallas_call | solution.py:645
  136.6 0.0 copy-start
  136.6 1.7 %copy.13 = f32[512,128]{1,0:T(8,128)} copy(f32[512,128]{1,0:T(8,128)} %get-tuple-element.4) | data formatting | bytes 524288
  138.3 0.0 copy-done
  138.3 0.7 copy.14
Async XLA Ops:
  136.6 1.7 %copy-start = (f32[512,128]{1,0:T(8,128)S(1)}, f32[512,128]{1,0:T(8,128)}, u32[]{:S(2)}) copy-start(f32[512,128]{1,0:T(8,128)} %get-tuple-element.5) | copy-start | bytes 786436

commit v5 on v4

--- a/solution.py
+++ b/solution.py
@@ -10,7 +10,7 @@
 MESH = pl.DeviceIdType.MESH
 ITERS = 2
 CHAINS = 2
-GROUP = 8
+GROUP = 16
 SCALE = 2.6857913
 FINE = 2896.0
 COARSE = 256.0
@@ -120,6 +120,10 @@
     odd = ((sh * 2 + 1) * 4 + sy) * 4 + sx
     meta_own[6:7, :] = jnp.where(index % 2 == 0, even, odd)
 
+    for k in range(2):
+        src_own[0, k] = sd[k * tile:(k + 1) * tile, :].astype(F32).T.astype(BF16)
+        s_mass[k] = sm[k * tile:(k + 1) * tile, :].T
+
     pl.semaphore_wait(barrier, len(friends))
 
     points_out = remote(tp, tp_in, p_send.at[0], p_recv.at[0], sibling)
@@ -187,17 +191,11 @@
                        s_band.at[it, 2 * r:2 * r + 2, rows_of(h)], s_send.at[h, 0],
                        s_recv.at[it, h, r], sibling).wait_recv()
 
-    for k in range(2):
-        src_own[0, k] = sd[k * tile:(k + 1) * tile, :].astype(F32).T.astype(BF16)
     for h in range(CHAINS):
         source_send(0, h)
 
-    for h in range(CHAINS):
-        source_pass_on(0, h)
-
     @pl.when(swapped)
     def _():
-        tm_copy.start()
         meta_copy.wait_recv()
         sp_copy.wait_recv()
         points_out.wait_recv()
@@ -218,26 +216,48 @@
 
     to_scalar.wait()
 
-    @pl.loop(0, slots)
-    def _(s):
+    acc[slots] = jnp.zeros((measures, tile), F32)
+
+    def make_tile(s):
         r, c = meta[0, s], meta[1, s]
         for part_at in range(tile // 128):
             lanes = slice(part_at * 128, (part_at + 1) * 128)
             distance = (sb[c, 0] - tt[r, 0:1, lanes]) ** 2
             distance = distance + (sb[c, 1] - tt[r, 1:2, lanes]) ** 2
             distance = distance + (sb[c, 2] - tt[r, 2:3, lanes]) ** 2
-            weight = jnp.exp2(-8.0 - distance)
-            kt[s, :, part_at * 128:(part_at + 1) * 128] = weight.astype(BF16)
-
-    acc[slots] = jnp.zeros((measures, tile), F32)
+            kt[s, :, lanes] = jnp.exp2(-8.0 - distance).astype(BF16)
+
+    def row_product(it, s):
+        acc[s] = acc[meta[2, s]] + jnp.dot(s_band[it, meta[1, s]], kt[s],
+                                           preferred_element_type=F32)
+
+    steps = 14
+    first_tiles = slots - 2 * steps
+
+    @pl.loop(0, first_tiles // 2)
+    def _(pair):
+        make_tile(2 * pair)
+        make_tile(2 * pair + 1)
+
+    for h in range(CHAINS):
+        source_pass_on(0, h)
 
     @pl.when(swapped)
     def _():
-        tm_copy.wait_recv()
-
-    for k in range(2):
-        t_mass[k] = tm_in[k * tile:(k + 1) * tile, :].T
-        s_mass[k] = sm[k * tile:(k + 1) * tile, :].T
+        tm_copy.start()
+
+    for h in range(CHAINS):
+        source_arrived(0, h)
+
+    @pl.loop(0, steps)
+    def _(step):
+        for m in range(3):
+            row_product(0, 3 * step + m)
+        for m in range(2):
+            make_tile(first_tiles + 2 * step + m)
+
+    for s in range(3 * steps, slots):
+        row_product(0, s)
 
     def write_block(ref, value):
         line = lax.broadcasted_iota(I32, (16, tile), 0)
@@ -265,13 +285,6 @@
         g = (place[a][0] + d) % 4
         gx, gy = (g, u) if a == 0 else (u, g)
         return meta[4, 2 * (gx * 8 + side * 4 + gy) + a]
-
-    def products(one, link):
-        @pl.loop(0, slots // GROUP)
-        def _(group):
-            for m in range(GROUP):
-                s = group * GROUP + m
-                acc[s] = one(s) + acc[meta[link, s]]
 
     class Chain:
         def __init__(self, h, it):
@@ -317,13 +330,15 @@
             remote(ref, ref, q_send.at[self.h, a, kind],
                    q_recv.at[self.it, self.h, a, kind], sibling).wait_recv()
 
-        def pair(self, a, g, part_at):
-            return t_band.at[self.it, pl.ds(self.spot(a, g, 2 * part_at), 2), self.rows]
+        def pair(self, a, g, far):
+            q = place[a][1]
+            begin = 2 * (1 - q // 2) if far else 2 * (q // 2)
+            return t_band.at[self.it, pl.ds(self.spot(a, g, begin), 2), self.rows]
 
         def g_copy(self, a, kind):
             p = place[a][0]
             g = (p, p, p, p, (p + 3) % 4, (p + 1) % 4)[kind]
-            ref = self.pair(a, g, (0, 1, 0, 1, 0, 1)[kind])
+            ref = self.pair(a, g, kind % 2 == 1)
             return remote(ref, ref, g_send.at[self.h, a, kind], g_recv.at[self.it, self.h, a, kind],
                           on_ring(a, (1, 1, 3, 3, 1, 3)[kind]))
 
@@ -331,7 +346,7 @@
             p = place[a][0]
             g = ((p + 3) % 4, (p + 3) % 4, (p + 1) % 4, (p + 1) % 4,
                  (p + 2) % 4, (p + 2) % 4)[kind]
-            ref = self.pair(a, g, (0, 1, 0, 1, 0, 1)[kind])
+            ref = self.pair(a, g, kind % 2 == 1)
             remote(ref, ref, g_send.at[self.h, a, kind], g_recv.at[self.it, self.h, a, kind],
                    sibling).wait_recv()
 
@@ -462,20 +477,22 @@
                 self.q_copy(a, 2).start()
                 self.q_got(a, 1)
                 self.q_copy(a, 3).start()
+                self.g_copy(a, 0).start()
+                self.g_copy(a, 2).start()
 
         def gather_block(self):
             for a in range(2):
                 self.q_got(a, 2)
                 self.q_got(a, 3)
-                for kind in (0, 3, 1, 2):
-                    self.g_copy(a, kind).start()
-            for a in range(2):
-                self.c_copy(a, 0).start()
-
-        def gather_relay(self):
-            for a in range(2):
+                self.g_copy(a, 3).start()
+                self.g_copy(a, 1).start()
                 self.g_got(a, 0)
                 self.g_copy(a, 4).start()
+            for a in range(2):
+                self.c_copy(a, 0).start()
+
+        def gather_relay(self):
+            for a in range(2):
                 self.g_got(a, 3)
                 self.g_copy(a, 5).start()
             for a in range(2):
@@ -572,10 +589,17 @@
 
     def iteration(it, _):
         chains = [Chain(h, it) for h in range(CHAINS)]
-        for h in range(CHAINS):
-            source_arrived(it, h)
-        products(lambda s: jnp.dot(s_band[it, meta[1, s]], kt[s],
-                                   preferred_element_type=F32), 2)
+
+        @pl.when(it > 0)
+        def _():
+            for h in range(CHAINS):
+                source_arrived(1, h)
+
+            @pl.loop(0, slots // GROUP)
+            def _(group):
+                for m in range(GROUP):
+                    row_product(1, group * GROUP + m)
+
         for d in (2, 1, 3, 0):
             for chain in chains:
                 chain.stage(d)
@@ -584,6 +608,15 @@
                      "gather_last"):
             for chain in chains:
                 getattr(chain, name)()
+            if name == "ring_near":
+                @pl.when(it == 0)
+                def _():
+                    @pl.when(swapped)
+                    def _():
+                        tm_copy.wait_recv()
+
+                    for k in range(2):
+                        t_mass[k] = tm_in[k * tile:(k + 1) * tile, :].T
 
         @pl.when(it == ITERS - 1)
         def _():
@@ -600,9 +633,15 @@
 
         for chain in chains:
             chain.gathered()
-        products(lambda s: lax.dot_general(t_band[it, meta[6, s]], kt[s],
-                                           (((1,), (1,)), ((), ())),
-                                           preferred_element_type=F32), 3)
+
+        @pl.loop(0, slots // GROUP)
+        def _(group):
+            for m in range(GROUP):
+                s = group * GROUP + m
+                acc[s] = acc[meta[3, s]] + lax.dot_general(
+                    t_band[it, meta[6, s]], kt[s], (((1,), (1,)), ((), ())),
+                    preferred_element_type=F32)
+
         for name in ("to_owner", "to_owner_relay", "source"):
             for chain in chains:
                 getattr(chain, name)()

time: 139 us -> 137 us (0.986)
  Pallas kernels: 135 us -> 133 us
    pallas_call x1, Pallas kernels: 135 us -> 133 us  [local(): pl.pallas_call(functools.partial(kernel, slots), out_shape=(jax.ShapeDtyp...]
where the time goes in v5:
time: 137 us
  Pallas kernels  133 us (97%)
  local copies, waits for them, and re-layouts  2.42 us (2%)
    pallas_call x1, Pallas kernels, local(): pl.pallas_call(functools.partial(kernel, slots), out_shape=(jax.ShapeDtyp...  133 us

profile of v5, /device:TPU:1, one launch (start us, length us, event | category | flops | bytes accessed | tf_op | source)
XLA Modules:
  0.0 136.8 jit_solution(14072693650108702118)
XLA Ops:
  1.3 133.1 %shard_map.95 = (f32[512,128]{1,0:T(8,128)}, f32[512,128]{1,0:T(8,128)}) custom-call(f32[3,16384]{1,0:T(4,128)} %tp.1, f32[3,2048]{1,0:T(4,128)} %sp.1, f32[512,128]{1,0:T(8,128)} %tm.1, f32[512,128]{1,0:T(8,128)} %sm.1, bf16[512,128]{1,0:T(8,128)(2,1)} %sd.1, s32[1,48]{1,0:T(1,128)} %bitcast.2, s32[1,48]{1,0:T(1,128)} %bitcast.3, s32[1]{0:T(128)S(6)} %copy.12.tn), custom_call_target="tpu_custom_call" | custom-call | tf_op jit(solution)/shard_map/pallas_call | solution.py:684
  134.4 0.0 copy-start
  134.4 1.7 %copy.13 = f32[512,128]{1,0:T(8,128)} copy(f32[512,128]{1,0:T(8,128)} %get-tuple-element.4) | data formatting | bytes 524288
  136.1 0.0 copy-done
  136.1 0.7 copy.14
Async XLA Ops:
  134.4 1.7 %copy-start = (f32[512,128]{1,0:T(8,128)S(1)}, f32[512,128]{1,0:T(8,128)}, u32[]{:S(2)}) copy-start(f32[512,128]{1,0:T(8,128)} %get-tuple-element.5) | copy-start | bytes 786436

commit v6 on v5

--- a/solution.py
+++ b/solution.py
@@ -23,9 +23,8 @@
 def encode(x):
     level = jnp.log(jnp.maximum(x, 1e-37))
     ref = (level[0:1] * COARSE + 32768.5).astype(I32) - 32768
-    fine = (level - ref.astype(F32) * (1.0 / COARSE)) * FINE + 32768.5
-    code = jnp.clip(fine, 0.5, 65535.0).astype(I32) - 32768
-    return code.astype(I16), ref
+    fine = level * FINE + (32768.5 - ref.astype(F32) * (FINE / COARSE))
+    return (fine.astype(I32) - 32768).astype(I16), ref
 
 
 def decode(code, ref):
@@ -39,7 +38,7 @@
     tp, sp, tm, sm, sd, tr, tc, tn,
     td_out, so_out,
     meta_own, meta_in, meta, tp_in, sp_in, tm_in, tt, sb, kt, acc,
-    src_own, s_band, x0_send, x0_recv, r1_send, r1_recv, r2_send, r2_recv, part,
+    src_own, s_band, x0_send, x0_recv, r1_send, r1_recv, r2_recv, part,
     t_band, z_send, z_recv, td_own, t_mass, s_mass, t_all, s_all,
     p_send, p_recv, s_send, s_recv, x_send, x_recv, a_send, a_recv, b_send, b_recv,
     q_send, q_recv, g_send, g_recv, c_send, c_recv, w_send, w_recv, o_send, o_recv, m_sem,
@@ -62,8 +61,8 @@
     sibling = device(x, y, z, other)
     partner = device(x, y, core * 2 + z_lo, z_hi)
 
-    ring = {(0, step): device((x + step) % 4, y, z, core) for step in (1, 3)}
-    ring.update({(1, step): device(x, (y + step) % 4, z, core) for step in (1, 3)})
+    ring = {(0, step): device((x + step) % 4, y, z, core) for step in (1, 2, 3)}
+    ring.update({(1, step): device(x, (y + step) % 4, z, core) for step in (1, 2, 3)})
 
     def on_ring(axis, step):
         return ring[axis, step]
@@ -94,7 +93,7 @@
     barrier = pltpu.get_barrier_semaphore()
     friends = [device(x, y, (z + dz) % 4, (core + dk) % 2)
                for dz in range(4) for dk in range(2) if dz or dk]
-    friends += [on_ring(axis, step) for axis in (0, 1) for step in (1, 3)]
+    friends += [on_ring(axis, step) for axis in (0, 1) for step in (1, 2, 3)]
     for friend in friends:
         pl.semaphore_signal(barrier, inc=1, device_id=friend, device_id_type=MESH)
 
@@ -260,25 +259,17 @@
         row_product(0, s)
 
     def write_block(ref, value):
+        coded = [encode(value(i)) for i in range(2)]
+        for i in range(2):
+            ref[i * mh:(i + 1) * mh, :] = coded[i][0]
         line = lax.broadcasted_iota(I32, (16, tile), 0)
-
-        def piece(i, refs):
-            code, ref_row = encode(value(i))
-            ref[pl.ds(pl.multiple_of(i * mh, 16), mh), :] = code
-            return jnp.where(line == i, ref_row, refs)
-
-        refs = lax.fori_loop(0, 2, piece, jnp.zeros((16, tile), I32))
-        ref[2 * mh:2 * mh + 16, :] = refs.astype(I16)
+        ref[2 * mh:2 * mh + 16, :] = jnp.where(line == 0, coded[0][1], coded[1][1]).astype(I16)
 
     def read_block(ref, i):
         refs = ref[2 * mh:2 * mh + 16, :].astype(I32)
-        line = lax.broadcasted_iota(I32, (16, tile), 0)
-        ref_row = jnp.sum(jnp.where(line == i, refs, 0), axis=0, keepdims=True)
-        return decode(ref[pl.ds(pl.multiple_of(i * mh, 16), mh), :], ref_row)
+        return decode(ref[i * mh:(i + 1) * mh, :], refs[i:i + 1])
 
     place = ((x, y), (y, x))
-    half = mh // 2
-    lower, upper, full = slice(0, half), slice(half, mh), slice(0, mh)
     out_copy = remote(td_own, td_out, o_send, o_recv, partner)
 
     def total(a, d, u, side):
@@ -302,31 +293,22 @@
                           on_ring(a, 1 if kind % 2 == 0 else 3))
 
         def r2_copy(self, a, kind):
-            h, it = self.h, self.it
-            return remote(r2_send.at[h, a, kind], r2_recv.at[it, h, a, kind],
-                          b_send.at[h, a, kind], b_recv.at[it, h, a, kind],
-                          on_ring(1 - a, 1 if kind % 2 == 0 else 3))
+            h, it, step = self.h, self.it, (1, 3, 2)[kind]
+            return remote(part.at[h, a, (place[a][1] + step) % 4], r2_recv.at[it, h, a, kind],
+                          b_send.at[h, a, kind], b_recv.at[it, h, a, kind], on_ring(1 - a, step))
 
         def spot(self, a, g, u, side=None):
             return (((core if side is None else side) * 2 + a) * 4 + g) * 4 + u
 
-        def some(self, kind):
-            begin = self.h * mh
-            return (self.rows, self.rows, slice(begin, begin + half),
-                    slice(begin + half, begin + mh))[kind]
-
         def q_copy(self, a, kind):
             p, q = place[a]
-            u = (q, q, (q + 3) % 4, (q + 1) % 4)[kind]
-            ref = t_band.at[self.it, self.spot(a, p, u), self.some(kind)]
+            ref = t_band.at[self.it, self.spot(a, p, q), self.rows]
             return remote(ref, ref, q_send.at[self.h, a, kind],
-                          q_recv.at[self.it, self.h, a, kind],
-                          on_ring(1 - a, 1 if kind % 2 == 0 else 3))
+                          q_recv.at[self.it, self.h, a, kind], on_ring(1 - a, (1, 3, 2)[kind]))
 
         def q_got(self, a, kind):
             p, q = place[a]
-            u = ((q + 3) % 4, (q + 1) % 4, (q + 2) % 4, (q + 2) % 4)[kind]
-            ref = t_band.at[self.it, self.spot(a, p, u), self.some(kind)]
+            ref = t_band.at[self.it, self.spot(a, p, (q + (3, 1, 2)[kind]) % 4), self.rows]
             remote(ref, ref, q_send.at[self.h, a, kind],
                    q_recv.at[self.it, self.h, a, kind], sibling).wait_recv()
 
@@ -424,8 +406,7 @@
                 self.r1_copy(a, 2).wait_recv()
                 self.r1_copy(a, 3).wait_recv()
 
-                @pl.loop(0, 2)
-                def _(i):
+                for i in range(2):
                     part[h, a, i] = self.own(a, 0, i) + read_block(r1_recv.at[it, h, a, 3], i)
                     part[h, a, 2 + i] = self.own(a, 0, 2 + i) + read_block(
                         r1_recv.at[it, h, a, 2], i)
@@ -433,57 +414,38 @@
         def ring_total(self):
             h, it = self.h, self.it
             for a in range(2):
-                q = place[a][1]
                 self.r1_copy(a, 4).wait_recv()
                 self.r1_copy(a, 5).wait_recv()
-
-                @pl.loop(0, 2)
-                def _(i):
+                for i in range(2):
                     part[h, a, i] += read_block(r1_recv.at[it, h, a, 4], i)
                     part[h, a, 2 + i] += read_block(r1_recv.at[it, h, a, 5], i)
-
-                for kind, d, side in ((0, 2, lower), (1, 2, upper), (2, 1, upper), (3, 3, lower)):
-                    r2_send[h, a, kind] = part[h, a, (q + d) % 4, side]
+                for kind in (2, 0, 1):
                     self.r2_copy(a, kind).start()
 
-        def short_relay(self):
-            h, it = self.h, self.it
-            for a in range(2):
-                q = place[a][1]
-                for kind, d, side in ((4, 1, lower), (5, 3, upper)):
-                    self.r2_copy(a, kind - 4).wait_recv()
-                    r2_send[h, a, kind] = (part[h, a, (q + d) % 4, side]
-                                           + r2_recv[it, h, a, kind - 4])
-                    self.r2_copy(a, kind).start()
-
         def target(self):
             h, it = self.h, self.it
             for a in range(2):
                 p, q = place[a]
-                for kind in (2, 3, 4, 5):
+                for kind in range(3):
                     self.r2_copy(a, kind).wait_recv()
-                sums = part[h, a, q] + jnp.concatenate(
-                    [r2_recv[it, h, a, 3] + r2_recv[it, h, a, 4],
-                     r2_recv[it, h, a, 2] + r2_recv[it, h, a, 5]], axis=0)
+                sums = (part[h, a, q] + r2_recv[it, h, a, 0]) + (
+                    r2_recv[it, h, a, 1] + r2_recv[it, h, a, 2])
                 dual = t_mass[a, self.rows] / sums
                 t_band[it, self.spot(a, p, q), self.rows] = dual.astype(BF16)
-                self.q_copy(a, 0).start()
-                self.q_copy(a, 1).start()
+                for kind in (2, 0, 1):
+                    self.q_copy(a, kind).start()
                 t_all[a, self.rows] = dual
 
         def gather_near(self):
             for a in range(2):
                 self.q_got(a, 0)
-                self.q_copy(a, 2).start()
                 self.q_got(a, 1)
-                self.q_copy(a, 3).start()
                 self.g_copy(a, 0).start()
                 self.g_copy(a, 2).start()
 
         def gather_block(self):
             for a in range(2):
                 self.q_got(a, 2)
-                self.q_got(a, 3)
                 self.g_copy(a, 3).start()
                 self.g_copy(a, 1).start()
                 self.g_got(a, 0)
@@ -574,10 +536,11 @@
             for a in range(2):
                 for kind in range(6):
                     self.r1_copy(a, kind).wait_send()
+                    self.g_copy(a, kind).wait_send()
+                for kind in range(3):
                     self.r2_copy(a, kind).wait_send()
-                    self.g_copy(a, kind).wait_send()
+                    self.q_copy(a, kind).wait_send()
                 for kind in range(4):
-                    self.q_copy(a, kind).wait_send()
                     self.c_copy(a, kind).wait_send()
             first = 2 * (delta % 2)
             for at in range(2):
@@ -604,7 +567,7 @@
             for chain in chains:
                 chain.stage(d)
         for name in ("ring_far", "ring_near", "ring_relay", "ring_sum", "ring_total",
-                     "short_relay", "target", "gather_near", "gather_block", "gather_relay",
+                     "target", "gather_near", "gather_block", "gather_relay",
                      "gather_last"):
             for chain in chains:
                 getattr(chain, name)()
@@ -706,8 +669,7 @@
             vmem((CHAINS, 4, 2, 4, mh, tile), F32),
             vmem((CHAINS, 2, 6, block, tile), I16),
             vmem((ITERS, CHAINS, 2, 6, block, tile), I16),
-            vmem((CHAINS, 2, 6, mh // 2, tile), F32),
-            vmem((ITERS, CHAINS, 2, 6, mh // 2, tile), F32),
+            vmem((ITERS, CHAINS, 2, 3, mh, tile), F32),
             vmem((CHAINS, 2, 4, mh, tile), F32),
             vmem((ITERS, 64, measures, tile), BF16),
             vmem((CHAINS, 4, block, tile), I16),
@@ -721,8 +683,8 @@
             dma((CHAINS, 4)), dma((ITERS, CHAINS, 4)),
             dma((CHAINS, 4)), dma((ITERS, CHAINS, 4)),
             dma((CHAINS, 2, 6)), dma((ITERS, CHAINS, 2, 6)),
-            dma((CHAINS, 2, 6)), dma((ITERS, CHAINS, 2, 6)),
-            dma((CHAINS, 2, 4)), dma((ITERS, CHAINS, 2, 4)),
+            dma((CHAINS, 2, 3)), dma((ITERS, CHAINS, 2, 3)),
+            dma((CHAINS, 2, 3)), dma((ITERS, CHAINS, 2, 3)),
             dma((CHAINS, 2, 6)), dma((ITERS, CHAINS, 2, 6)),
             dma((CHAINS, 2, 4)), dma((ITERS, CHAINS, 2, 4)),
             dma((CHAINS, 4)), dma((ITERS, CHAINS, 4)),

time: 137 us -> 136 us (level)
  no operation moved by 1% of the time
where the time goes in v6:
time: 136 us
  Pallas kernels  132 us (97%)
  local copies, waits for them, and re-layouts  2.42 us (2%)
    pallas_call x1, Pallas kernels, local(): pl.pallas_call(functools.partial(kernel, slots), out_shape=(jax.ShapeDtyp...  132 us

profile of v6, /device:TPU:1, one launch (start us, length us, event | category | flops | bytes accessed | tf_op | source)
XLA Modules:
  0.0 135.7 jit_solution(8463326118345538928)
XLA Ops:
  1.3 132.0 %shard_map.95 = (f32[512,128]{1,0:T(8,128)}, f32[512,128]{1,0:T(8,128)}) custom-call(f32[3,16384]{1,0:T(4,128)} %tp.1, f32[3,2048]{1,0:T(4,128)} %sp.1, f32[512,128]{1,0:T(8,128)} %tm.1, f32[512,128]{1,0:T(8,128)} %sm.1, bf16[512,128]{1,0:T(8,128)(2,1)} %sd.1, s32[1,48]{1,0:T(1,128)} %bitcast.2, s32[1,48]{1,0:T(1,128)} %bitcast.3, s32[1]{0:T(128)S(6)} %copy.12.tn), custom_call_target="tpu_custom_call" | custom-call | tf_op jit(solution)/shard_map/pallas_call | solution.py:647
  133.3 0.0 copy-start
  133.3 1.7 %copy.13 = f32[512,128]{1,0:T(8,128)} copy(f32[512,128]{1,0:T(8,128)} %get-tuple-element.4) | data formatting | bytes 524288
  135.0 0.0 copy-done
  135.0 0.7 copy.14
Async XLA Ops:
  133.3 1.7 %copy-start = (f32[512,128]{1,0:T(8,128)S(1)}, f32[512,128]{1,0:T(8,128)}, u32[]{:S(2)}) copy-start(f32[512,128]{1,0:T(8,128)} %get-tuple-element.5) | copy-start | bytes 786436

commit v7 on v6

--- a/solution.py
+++ b/solution.py
@@ -258,15 +258,17 @@
     for s in range(3 * steps, slots):
         row_product(0, s)
 
-    def write_block(ref, value):
-        coded = [encode(value(i)) for i in range(2)]
-        for i in range(2):
-            ref[i * mh:(i + 1) * mh, :] = coded[i][0]
+    def write_block(ref, value, n=2):
         line = lax.broadcasted_iota(I32, (16, tile), 0)
-        ref[2 * mh:2 * mh + 16, :] = jnp.where(line == 0, coded[0][1], coded[1][1]).astype(I16)
-
-    def read_block(ref, i):
-        refs = ref[2 * mh:2 * mh + 16, :].astype(I32)
+        refs = jnp.zeros((16, tile), I32)
+        for i in range(n):
+            code, ref_row = encode(value(i))
+            ref[i * mh:(i + 1) * mh, :] = code
+            refs = jnp.where(line == i, ref_row, refs)
+        ref[n * mh:n * mh + 16, :] = refs.astype(I16)
+
+    def read_block(ref, i, n=2):
+        refs = ref[n * mh:n * mh + 16, :].astype(I32)
         return decode(ref[i * mh:(i + 1) * mh, :], refs[i:i + 1])
 
     place = ((x, y), (y, x))
@@ -366,14 +368,12 @@
                 fn(self.z_copy(2, r))
 
         def own(self, a, d, u):
-            return acc[total(a, d, u, core), self.rows] + x0_recv[self.h, d, a, u]
+            return acc[total(a, d, u, core), self.rows] + read_block(
+                x0_recv.at[self.h, d], a * 4 + u, 8)
 
         def stage(self, d):
-            for a in range(2):
-                @pl.loop(0, 4)
-                def _(u):
-                    x0_send[self.h, d, a, u] = acc[total(a, d, u, other), self.rows]
-
+            write_block(x0_send.at[self.h, d],
+                        lambda i: acc[total(i // 4, d, i % 4, other), self.rows], 8)
             self.x0_copy(d).start()
 
         def ring_far(self):
@@ -563,14 +563,19 @@
                 for m in range(GROUP):
                     row_product(1, group * GROUP + m)
 
-        for d in (2, 1, 3, 0):
-            for chain in chains:
-                chain.stage(d)
+        for chain in chains:
+            chain.stage(2)
+        for chain in chains:
+            chain.stage(1)
+            chain.stage(3)
         for name in ("ring_far", "ring_near", "ring_relay", "ring_sum", "ring_total",
                      "target", "gather_near", "gather_block", "gather_relay",
                      "gather_last"):
             for chain in chains:
                 getattr(chain, name)()
+            if name == "ring_far":
+                for chain in chains:
+                    chain.stage(0)
             if name == "ring_near":
                 @pl.when(it == 0)
                 def _():
@@ -665,8 +670,8 @@
             vmem((slots + 1, measures, tile), F32),
             vmem((ITERS, 2, measures, tile), BF16),
             vmem((ITERS, 8, measures, tile), BF16),
-            vmem((CHAINS, 4, 2, 4, mh, tile), F32),
-            vmem((CHAINS, 4, 2, 4, mh, tile), F32),
+            vmem((CHAINS, 4, 8 * mh + 16, tile), I16),
+            vmem((CHAINS, 4, 8 * mh + 16, tile), I16),
             vmem((CHAINS, 2, 6, block, tile), I16),
             vmem((ITERS, CHAINS, 2, 6, block, tile), I16),
             vmem((ITERS, CHAINS, 2, 3, mh, tile), F32),

time: 136 us -> 137 us (level)
  no operation moved by 1% of the time
where the time goes in v7:
time: 137 us; the launch traced here: 136 us
  Pallas kernels  133 us (97%)
  local copies, waits for them, and re-layouts  2.42 us (2%)
    pallas_call x1, Pallas kernels, local(): pl.pallas_call(functools.partial(kernel, slots), out_shape=(jax.ShapeDtyp...  133 us

profile of v7, /device:TPU:1, one launch (start us, length us, event | category | flops | bytes accessed | tf_op | source)
XLA Modules:
  0.0 136.5 jit_solution(5330559074519081164)
XLA Ops:
  1.3 132.8 %shard_map.95 = (f32[512,128]{1,0:T(8,128)}, f32[512,128]{1,0:T(8,128)}) custom-call(f32[3,16384]{1,0:T(4,128)} %tp.1, f32[3,2048]{1,0:T(4,128)} %sp.1, f32[512,128]{1,0:T(8,128)} %tm.1, f32[512,128]{1,0:T(8,128)} %sm.1, bf16[512,128]{1,0:T(8,128)(2,1)} %sd.1, s32[1,48]{1,0:T(1,128)} %bitcast.2, s32[1,48]{1,0:T(1,128)} %bitcast.3, s32[1]{0:T(128)S(6)} %copy.12.tn), custom_call_target="tpu_custom_call" | custom-call | tf_op jit(solution)/shard_map/pallas_call | solution.py:652
  134.0 0.0 copy-start
  134.1 1.7 %copy.13 = f32[512,128]{1,0:T(8,128)} copy(f32[512,128]{1,0:T(8,128)} %get-tuple-element.4) | data formatting | bytes 524288
  135.8 0.0 copy-done
  135.8 0.7 copy.14
Async XLA Ops:
  134.0 1.7 %copy-start = (f32[512,128]{1,0:T(8,128)S(1)}, f32[512,128]{1,0:T(8,128)}, u32[]{:S(2)}) copy-start(f32[512,128]{1,0:T(8,128)} %get-tuple-element.5) | copy-start | bytes 786436

commit v8 on v6

--- a/solution.py
+++ b/solution.py
@@ -38,7 +38,7 @@
     tp, sp, tm, sm, sd, tr, tc, tn,
     td_out, so_out,
     meta_own, meta_in, meta, tp_in, sp_in, tm_in, tt, sb, kt, acc,
-    src_own, s_band, x0_send, x0_recv, r1_send, r1_recv, r2_recv, part,
+    src_own, s_band, x0_send, x0_recv, r1_send, r1_recv, r2_send, r2_recv, part,
     t_band, z_send, z_recv, td_own, t_mass, s_mass, t_all, s_all,
     p_send, p_recv, s_send, s_recv, x_send, x_recv, a_send, a_recv, b_send, b_recv,
     q_send, q_recv, g_send, g_recv, c_send, c_recv, w_send, w_recv, o_send, o_recv, m_sem,
@@ -258,15 +258,18 @@
     for s in range(3 * steps, slots):
         row_product(0, s)
 
-    def write_block(ref, value):
-        coded = [encode(value(i)) for i in range(2)]
-        for i in range(2):
-            ref[i * mh:(i + 1) * mh, :] = coded[i][0]
+    def write_block(ref, values):
+        n = len(values)
         line = lax.broadcasted_iota(I32, (16, tile), 0)
-        ref[2 * mh:2 * mh + 16, :] = jnp.where(line == 0, coded[0][1], coded[1][1]).astype(I16)
-
-    def read_block(ref, i):
-        refs = ref[2 * mh:2 * mh + 16, :].astype(I32)
+        refs = jnp.zeros((16, tile), I32)
+        for i in range(n):
+            code, ref_row = encode(values[i]())
+            ref[i * mh:(i + 1) * mh, :] = code
+            refs = jnp.where(line == i, ref_row, refs)
+        ref[n * mh:n * mh + 16, :] = refs.astype(I16)
+
+    def read_block(ref, i, n=2):
+        refs = ref[n * mh:n * mh + 16, :].astype(I32)
         return decode(ref[i * mh:(i + 1) * mh, :], refs[i:i + 1])
 
     place = ((x, y), (y, x))
@@ -286,15 +289,18 @@
             return remote(x0_send.at[h, d], x0_recv.at[h, d], x_send.at[h, d],
                           x_recv.at[self.it, h, d], sibling)
 
+        def r1_rows(self, kind):
+            return slice(0, (4 if kind < 2 else 2) * mh + 16)
+
         def r1_copy(self, a, kind):
-            h, it = self.h, self.it
-            return remote(r1_send.at[h, a, kind], r1_recv.at[it, h, a, kind],
+            h, it, rows = self.h, self.it, self.r1_rows(kind)
+            return remote(r1_send.at[h, a, kind, rows], r1_recv.at[it, h, a, kind, rows],
                           a_send.at[h, a, kind], a_recv.at[it, h, a, kind],
                           on_ring(a, 1 if kind % 2 == 0 else 3))
 
         def r2_copy(self, a, kind):
             h, it, step = self.h, self.it, (1, 3, 2)[kind]
-            return remote(part.at[h, a, (place[a][1] + step) % 4], r2_recv.at[it, h, a, kind],
+            return remote(r2_send.at[h, a, kind], r2_recv.at[it, h, a, kind],
                           b_send.at[h, a, kind], b_recv.at[it, h, a, kind], on_ring(1 - a, step))
 
         def spot(self, a, g, u, side=None):
@@ -376,50 +382,49 @@
 
             self.x0_copy(d).start()
 
-        def ring_far(self):
-            self.x0_copy(2).wait_recv()
-            for a in range(2):
-                for kind, d, u0 in ((0, 2, 0), (1, 2, 2)):
-                    write_block(r1_send.at[self.h, a, kind], lambda i: self.own(a, d, u0 + i))
+        def ring_first(self):
+            for d in (2, 1, 3):
+                self.x0_copy(d).wait_recv()
+            for a in range(2):
+                for kind, d, far, near in ((0, 1, 0, 2), (1, 3, 2, 0)):
+                    write_block(r1_send.at[self.h, a, kind],
+                                [functools.partial(self.own, a, 2, far + i) for i in range(2)]
+                                + [functools.partial(self.own, a, d, near + i) for i in range(2)])
                     self.r1_copy(a, kind).start()
 
-        def ring_near(self):
-            for kind, d, u0 in ((2, 1, 2), (3, 3, 0)):
-                self.x0_copy(d).wait_recv()
-                for a in range(2):
-                    write_block(r1_send.at[self.h, a, kind], lambda i: self.own(a, d, u0 + i))
+        def ring_relay(self):
+            h, it = self.h, self.it
+            for a in range(2):
+                for kind, d, u0 in ((2, 1, 0), (3, 3, 2)):
+                    self.r1_copy(a, kind - 2).wait_recv()
+                    got = r1_recv.at[it, h, a, kind - 2]
+                    write_block(r1_send.at[h, a, kind],
+                                [lambda i=i: self.own(a, d, u0 + i) + read_block(got, i, 4)
+                                 for i in range(2)])
                     self.r1_copy(a, kind).start()
 
-        def ring_relay(self):
-            for a in range(2):
-                for kind, d, u0 in ((4, 1, 0), (5, 3, 2)):
-                    self.r1_copy(a, kind - 4).wait_recv()
-                    got = r1_recv.at[self.it, self.h, a, kind - 4]
-                    write_block(r1_send.at[self.h, a, kind],
-                                lambda i: self.own(a, d, u0 + i) + read_block(got, i))
-                    self.r1_copy(a, kind).start()
-
         def ring_sum(self):
             h, it = self.h, self.it
             self.x0_copy(0).wait_recv()
             for a in range(2):
+                for i in range(2):
+                    part[h, a, i] = self.own(a, 0, i) + read_block(
+                        r1_recv.at[it, h, a, 1], 2 + i, 4)
+                    part[h, a, 2 + i] = self.own(a, 0, 2 + i) + read_block(
+                        r1_recv.at[it, h, a, 0], 2 + i, 4)
+
+        def ring_total(self):
+            h, it = self.h, self.it
+            for a in range(2):
+                q = place[a][1]
                 self.r1_copy(a, 2).wait_recv()
                 self.r1_copy(a, 3).wait_recv()
-
                 for i in range(2):
-                    part[h, a, i] = self.own(a, 0, i) + read_block(r1_recv.at[it, h, a, 3], i)
-                    part[h, a, 2 + i] = self.own(a, 0, 2 + i) + read_block(
-                        r1_recv.at[it, h, a, 2], i)
-
-        def ring_total(self):
-            h, it = self.h, self.it
-            for a in range(2):
-                self.r1_copy(a, 4).wait_recv()
-                self.r1_copy(a, 5).wait_recv()
-                for i in range(2):
-                    part[h, a, i] += read_block(r1_recv.at[it, h, a, 4], i)
-                    part[h, a, 2 + i] += read_block(r1_recv.at[it, h, a, 5], i)
+                    part[h, a, i] += read_block(r1_recv.at[it, h, a, 2], i)
+                    part[h, a, 2 + i] += read_block(r1_recv.at[it, h, a, 3], i)
                 for kind in (2, 0, 1):
+                    write_block(r2_send.at[h, a, kind],
+                                [lambda: part[h, a, (q + (1, 3, 2)[kind]) % 4]])
                     self.r2_copy(a, kind).start()
 
         def target(self):
@@ -428,8 +433,9 @@
                 p, q = place[a]
                 for kind in range(3):
                     self.r2_copy(a, kind).wait_recv()
-                sums = (part[h, a, q] + r2_recv[it, h, a, 0]) + (
-                    r2_recv[it, h, a, 1] + r2_recv[it, h, a, 2])
+                sums = part[h, a, q]
+                for kind in range(3):
+                    sums = sums + read_block(r2_recv.at[it, h, a, kind], 0, 1)
                 dual = t_mass[a, self.rows] / sums
                 t_band[it, self.spot(a, p, q), self.rows] = dual.astype(BF16)
                 for kind in (2, 0, 1):
@@ -479,7 +485,8 @@
             first = 2 * (delta % 2)
             for at in range(2):
                 r = first + at
-                write_block(z_send.at[h, r], lambda i: acc[meta[5, 2 * r + i], self.rows])
+                write_block(z_send.at[h, r],
+                            [lambda i=i: acc[meta[5, 2 * r + i], self.rows] for i in range(2)])
 
                 @pl.when(swapped)
                 def _():
@@ -494,7 +501,8 @@
                 def _():
                     z_recv[it, h, 0] = z_send[h, r]
 
-            write_block(z_send.at[h, single], lambda i: acc[meta[5, 2 * single + i], self.rows])
+            write_block(z_send.at[h, single],
+                        [lambda i=i: acc[meta[5, 2 * single + i], self.rows] for i in range(2)])
             self.to_next(single, lambda copy: copy.start())
 
         def to_owner_relay(self):
@@ -502,7 +510,8 @@
             self.z_far(0, sibling).wait_recv()
             got = z_recv.at[it, h, 3]
             write_block(z_send.at[h, relayed],
-                        lambda i: acc[meta[5, 2 * relayed + i], self.rows] + read_block(got, i))
+                        [lambda i=i: acc[meta[5, 2 * relayed + i], self.rows]
+                         + read_block(got, i) for i in range(2)])
             self.to_next(relayed, lambda copy: copy.start())
 
         def source(self):
@@ -534,8 +543,9 @@
             for d in range(4):
                 self.x0_copy(d).wait_send()
             for a in range(2):
+                for kind in range(4):
+                    self.r1_copy(a, kind).wait_send()
                 for kind in range(6):
-                    self.r1_copy(a, kind).wait_send()
                     self.g_copy(a, kind).wait_send()
                 for kind in range(3):
                     self.r2_copy(a, kind).wait_send()
@@ -566,12 +576,12 @@
         for d in (2, 1, 3, 0):
             for chain in chains:
                 chain.stage(d)
-        for name in ("ring_far", "ring_near", "ring_relay", "ring_sum", "ring_total",
+        for name in ("ring_first", "ring_relay", "ring_sum", "ring_total",
                      "target", "gather_near", "gather_block", "gather_relay",
                      "gather_last"):
             for chain in chains:
                 getattr(chain, name)()
-            if name == "ring_near":
+            if name == "ring_first":
                 @pl.when(it == 0)
                 def _():
                     @pl.when(swapped)
@@ -667,9 +677,10 @@
             vmem((ITERS, 8, measures, tile), BF16),
             vmem((CHAINS, 4, 2, 4, mh, tile), F32),
             vmem((CHAINS, 4, 2, 4, mh, tile), F32),
-            vmem((CHAINS, 2, 6, block, tile), I16),
-            vmem((ITERS, CHAINS, 2, 6, block, tile), I16),
-            vmem((ITERS, CHAINS, 2, 3, mh, tile), F32),
+            vmem((CHAINS, 2, 4, 4 * mh + 16, tile), I16),
+            vmem((ITERS, CHAINS, 2, 4, 4 * mh + 16, tile), I16),
+            vmem((CHAINS, 2, 3, mh + 16, tile), I16),
+            vmem((ITERS, CHAINS, 2, 3, mh + 16, tile), I16),
             vmem((CHAINS, 2, 4, mh, tile), F32),
             vmem((ITERS, 64, measures, tile), BF16),
             vmem((CHAINS, 4, block, tile), I16),
@@ -682,7 +693,7 @@
             dma((4,)), dma((4,)),
             dma((CHAINS, 4)), dma((ITERS, CHAINS, 4)),
             dma((CHAINS, 4)), dma((ITERS, CHAINS, 4)),
-            dma((CHAINS, 2, 6)), dma((ITERS, CHAINS, 2, 6)),
+            dma((CHAINS, 2, 4)), dma((ITERS, CHAINS, 2, 4)),
             dma((CHAINS, 2, 3)), dma((ITERS, CHAINS, 2, 3)),
             dma((CHAINS, 2, 3)), dma((ITERS, CHAINS, 2, 3)),
             dma((CHAINS, 2, 6)), dma((ITERS, CHAINS, 2, 6)),

time: 136 us -> 133 us (0.978)
  Pallas kernels: 132 us -> 129 us
    pallas_call x1, Pallas kernels: 132 us -> 129 us  [local(): pl.pallas_call(functools.partial(kernel, slots), out_shape=(jax.ShapeDtyp...]
where the time goes in v8:
time: 133 us
  Pallas kernels  129 us (97%)
  local copies, waits for them, and re-layouts  2.42 us (2%)
    pallas_call x1, Pallas kernels, local(): pl.pallas_call(functools.partial(kernel, slots), out_shape=(jax.ShapeDtyp...  129 us

profile of v8, /device:TPU:1, one launch (start us, length us, event | category | flops | bytes accessed | tf_op | source)
XLA Modules:
  0.0 132.5 jit_solution(6588756676716582030)
XLA Ops:
  1.3 128.8 %shard_map.95 = (f32[512,128]{1,0:T(8,128)}, f32[512,128]{1,0:T(8,128)}) custom-call(f32[3,16384]{1,0:T(4,128)} %tp.1, f32[3,2048]{1,0:T(4,128)} %sp.1, f32[512,128]{1,0:T(8,128)} %tm.1, f32[512,128]{1,0:T(8,128)} %sm.1, bf16[512,128]{1,0:T(8,128)(2,1)} %sd.1, s32[1,48]{1,0:T(1,128)} %bitcast.2, s32[1,48]{1,0:T(1,128)} %bitcast.3, s32[1]{0:T(128)S(6)} %copy.12.tn), custom_call_target="tpu_custom_call" | custom-call | tf_op jit(solution)/shard_map/pallas_call | solution.py:657
  130.1 0.0 copy-start
  130.1 1.7 %copy.13 = f32[512,128]{1,0:T(8,128)} copy(f32[512,128]{1,0:T(8,128)} %get-tuple-element.4) | data formatting | bytes 524288
  131.8 0.0 copy-done
  131.8 0.7 copy.14
Async XLA Ops:
  130.1 1.7 %copy-start = (f32[512,128]{1,0:T(8,128)S(1)}, f32[512,128]{1,0:T(8,128)}, u32[]{:S(2)}) copy-start(f32[512,128]{1,0:T(8,128)} %get-tuple-element.5) | copy-start | bytes 786436

commit v9 on v8

--- a/solution.py
+++ b/solution.py
@@ -207,9 +207,10 @@
         start = pl.multiple_of(c * tile, tile)
         for k in range(3):
             line = sp_in[k:k + 1, pl.ds(start, tile)] * SCALE
-            sb[c, k] = jnp.broadcast_to(line, (128, tile)).T
-
-    @pl.loop(0, 64)
+            column = jnp.broadcast_to(line, (8, tile)).T[:, 0:1]
+            sb[c, k] = jnp.broadcast_to(column, (tile, 128))
+
+    @pl.loop(0, 64, unroll=8)
     def _(r):
         tt[r, 0:3] = tp_in[:, pl.ds(pl.multiple_of(r * tile, tile), tile)] * SCALE
 
@@ -383,10 +384,10 @@
             self.x0_copy(d).start()
 
         def ring_first(self):
-            for d in (2, 1, 3):
+            self.x0_copy(2).wait_recv()
+            for kind, d, far, near in ((0, 1, 0, 2), (1, 3, 2, 0)):
                 self.x0_copy(d).wait_recv()
-            for a in range(2):
-                for kind, d, far, near in ((0, 1, 0, 2), (1, 3, 2, 0)):
+                for a in range(2):
                     write_block(r1_send.at[self.h, a, kind],
                                 [functools.partial(self.own, a, 2, far + i) for i in range(2)]
                                 + [functools.partial(self.own, a, d, near + i) for i in range(2)])
@@ -573,15 +574,32 @@
                 for m in range(GROUP):
                     row_product(1, group * GROUP + m)
 
-        for d in (2, 1, 3, 0):
-            for chain in chains:
+        for chain in chains:
+            for d in (2, 1, 3):
                 chain.stage(d)
         for name in ("ring_first", "ring_relay", "ring_sum", "ring_total",
                      "target", "gather_near", "gather_block", "gather_relay",
                      "gather_last"):
             for chain in chains:
                 getattr(chain, name)()
+            if name == "gather_block":
+                @pl.when(it == ITERS - 1)
+                def _():
+                    for a in range(2):
+                        td_own[a * tile:(a + 1) * tile, :] = t_all[a].T
+
+                    @pl.when(swapped)
+                    def _():
+                        out_copy.start()
+
+                    @pl.when(own_role)
+                    def _():
+                        td_out[...] = td_own[...]
+
             if name == "ring_first":
+                for chain in chains:
+                    chain.stage(0)
+
                 @pl.when(it == 0)
                 def _():
                     @pl.when(swapped)
@@ -590,19 +608,6 @@
 
                     for k in range(2):
                         t_mass[k] = tm_in[k * tile:(k + 1) * tile, :].T
-
-        @pl.when(it == ITERS - 1)
-        def _():
-            for a in range(2):
-                td_own[a * tile:(a + 1) * tile, :] = t_all[a].T
-
-            @pl.when(swapped)
-            def _():
-                out_copy.start()
-
-            @pl.when(own_role)
-            def _():
-                td_out[...] = td_own[...]
 
         for chain in chains:
             chain.gathered()

time: 133 us -> 132 us (level)
  no operation moved by 1% of the time
where the time goes in v9:
time: 132 us
  Pallas kernels  128 us (97%)
  local copies, waits for them, and re-layouts  2.42 us (2%)
    pallas_call x1, Pallas kernels, local(): pl.pallas_call(functools.partial(kernel, slots), out_shape=(jax.ShapeDtyp...  128 us

profile of v9, /device:TPU:1, one launch (start us, length us, event | category | flops | bytes accessed | tf_op | source)
XLA Modules:
  0.0 131.9 jit_solution(10717804188518533755)
XLA Ops:
  1.3 128.2 %shard_map.95 = (f32[512,128]{1,0:T(8,128)}, f32[512,128]{1,0:T(8,128)}) custom-call(f32[3,16384]{1,0:T(4,128)} %tp.1, f32[3,2048]{1,0:T(4,128)} %sp.1, f32[512,128]{1,0:T(8,128)} %tm.1, f32[512,128]{1,0:T(8,128)} %sm.1, bf16[512,128]{1,0:T(8,128)(2,1)} %sd.1, s32[1,48]{1,0:T(1,128)} %bitcast.2, s32[1,48]{1,0:T(1,128)} %bitcast.3, s32[1]{0:T(128)S(6)} %copy.12.tn), custom_call_target="tpu_custom_call" | custom-call | tf_op jit(solution)/shard_map/pallas_call | solution.py:662
  129.5 0.0 copy-start
  129.5 1.7 %copy.13 = f32[512,128]{1,0:T(8,128)} copy(f32[512,128]{1,0:T(8,128)} %get-tuple-element.4) | data formatting | bytes 524288
  131.2 0.0 copy-done
  131.2 0.7 copy.14
Async XLA Ops:
  129.5 1.7 %copy-start = (f32[512,128]{1,0:T(8,128)S(1)}, f32[512,128]{1,0:T(8,128)}, u32[]{:S(2)}) copy-start(f32[512,128]{1,0:T(8,128)} %get-tuple-element.5) | copy-start | bytes 786436

commit v10 on v8

--- a/solution.py
+++ b/solution.py
@@ -149,12 +149,12 @@
     def source_copy(it, h, step):
         target = (sibling, up_band, None, down_band)[step]
         return remote(
-            src_own.at[it, :, rows_of(h)], s_band.at[it, pl.ds(2 * row, 2), rows_of(h)],
+            src_own.at[it, :, rows_of(h)], s_band[h].at[it, pl.ds(2 * row, 2)],
             s_send.at[h, step], s_recv.at[it, h, row], target,
         )
 
     def source_relay(it, h):
-        ref = s_band.at[it, pl.ds(2 * relayed, 2), rows_of(h)]
+        ref = s_band[h].at[it, pl.ds(2 * relayed, 2)]
         return remote(ref, ref, s_send.at[h, 2], s_recv.at[it, h, relayed], relay_on)
 
     def source_send(it, h):
@@ -167,7 +167,7 @@
 
         @pl.when(own_role)
         def _():
-            s_band[it, pl.ds(2 * row, 2), rows_of(h)] = src_own[it, :, rows_of(h)]
+            s_band[h][it, pl.ds(2 * row, 2)] = src_own[it, :, rows_of(h)]
 
     def source_sent(it, h):
         source_copy(it, h, 1).wait_send()
@@ -187,7 +187,7 @@
             @pl.when(jnp.logical_and(jnp.logical_or(swapped, row != r), relayed != r))
             def _():
                 remote(src_own.at[it, :, rows_of(h)],
-                       s_band.at[it, 2 * r:2 * r + 2, rows_of(h)], s_send.at[h, 0],
+                       s_band[h].at[it, 2 * r:2 * r + 2], s_send.at[h, 0],
                        s_recv.at[it, h, r], sibling).wait_recv()
 
     for h in range(CHAINS):
@@ -207,9 +207,10 @@
         start = pl.multiple_of(c * tile, tile)
         for k in range(3):
             line = sp_in[k:k + 1, pl.ds(start, tile)] * SCALE
-            sb[c, k] = jnp.broadcast_to(line, (128, tile)).T
-
-    @pl.loop(0, 64)
+            column = jnp.broadcast_to(line, (8, tile)).T[:, 0:1]
+            sb[c, k] = jnp.broadcast_to(column, (tile, 128))
+
+    @pl.loop(0, 64, unroll=8)
     def _(r):
         tt[r, 0:3] = tp_in[:, pl.ds(pl.multiple_of(r * tile, tile), tile)] * SCALE
 
@@ -226,9 +227,22 @@
             distance = distance + (sb[c, 2] - tt[r, 2:3, lanes]) ** 2
             kt[s, :, lanes] = jnp.exp2(-8.0 - distance).astype(BF16)
 
-    def row_product(it, s):
-        acc[s] = acc[meta[2, s]] + jnp.dot(s_band[it, meta[1, s]], kt[s],
-                                           preferred_element_type=F32)
+    def row_product(it, h, s):
+        rows = rows_of(h)
+        acc[s, rows] = acc[meta[2, s], rows] + jnp.dot(
+            s_band[h][it, meta[1, s]], kt[s], preferred_element_type=F32)
+
+    def column_product(it, h, s):
+        rows = rows_of(h)
+        acc[s, rows] = acc[meta[3, s], rows] + lax.dot_general(
+            t_band[h][it, meta[6, s]], kt[s], (((1,), (1,)), ((), ())),
+            preferred_element_type=F32)
+
+    def products(one, it, h):
+        @pl.loop(0, slots // GROUP)
+        def _(group):
+            for m in range(GROUP):
+                one(it, h, group * GROUP + m)
 
     steps = 14
     first_tiles = slots - 2 * steps
@@ -251,12 +265,14 @@
     @pl.loop(0, steps)
     def _(step):
         for m in range(3):
-            row_product(0, 3 * step + m)
+            for h in range(CHAINS):
+                row_product(0, h, 3 * step + m)
         for m in range(2):
             make_tile(first_tiles + 2 * step + m)
 
     for s in range(3 * steps, slots):
-        row_product(0, s)
+        for h in range(CHAINS):
+            row_product(0, h, s)
 
     def write_block(ref, values):
         n = len(values)
@@ -308,20 +324,20 @@
 
         def q_copy(self, a, kind):
             p, q = place[a]
-            ref = t_band.at[self.it, self.spot(a, p, q), self.rows]
+            ref = t_band[self.h].at[self.it, self.spot(a, p, q)]
             return remote(ref, ref, q_send.at[self.h, a, kind],
                           q_recv.at[self.it, self.h, a, kind], on_ring(1 - a, (1, 3, 2)[kind]))
 
         def q_got(self, a, kind):
             p, q = place[a]
-            ref = t_band.at[self.it, self.spot(a, p, (q + (3, 1, 2)[kind]) % 4), self.rows]
+            ref = t_band[self.h].at[self.it, self.spot(a, p, (q + (3, 1, 2)[kind]) % 4)]
             remote(ref, ref, q_send.at[self.h, a, kind],
                    q_recv.at[self.it, self.h, a, kind], sibling).wait_recv()
 
         def pair(self, a, g, far):
             q = place[a][1]
             begin = 2 * (1 - q // 2) if far else 2 * (q // 2)
-            return t_band.at[self.it, pl.ds(self.spot(a, g, begin), 2), self.rows]
+            return t_band[self.h].at[self.it, pl.ds(self.spot(a, g, begin), 2)]
 
         def g_copy(self, a, kind):
             p = place[a][0]
@@ -340,13 +356,13 @@
 
         def c_copy(self, a, dg):
             base = self.spot(a, (place[a][0] + dg) % 4, 0)
-            ref = t_band.at[self.it, pl.ds(base, 4), self.rows]
+            ref = t_band[self.h].at[self.it, pl.ds(base, 4)]
             return remote(ref, ref, c_send.at[self.h, a, dg],
                           c_recv.at[self.it, self.h, a, dg], sibling)
 
         def c_got(self, a, dg):
             base = self.spot(a, (place[a][0] + dg) % 4, 0, other)
-            ref = t_band.at[self.it, pl.ds(base, 4), self.rows]
+            ref = t_band[self.h].at[self.it, pl.ds(base, 4)]
             remote(ref, ref, c_send.at[self.h, a, dg],
                    c_recv.at[self.it, self.h, a, dg], sibling).wait_recv()
 
@@ -383,10 +399,10 @@
             self.x0_copy(d).start()
 
         def ring_first(self):
-            for d in (2, 1, 3):
+            self.x0_copy(2).wait_recv()
+            for kind, d, far, near in ((0, 1, 0, 2), (1, 3, 2, 0)):
                 self.x0_copy(d).wait_recv()
-            for a in range(2):
-                for kind, d, far, near in ((0, 1, 0, 2), (1, 3, 2, 0)):
+                for a in range(2):
                     write_block(r1_send.at[self.h, a, kind],
                                 [functools.partial(self.own, a, 2, far + i) for i in range(2)]
                                 + [functools.partial(self.own, a, d, near + i) for i in range(2)])
@@ -437,7 +453,7 @@
                 for kind in range(3):
                     sums = sums + read_block(r2_recv.at[it, h, a, kind], 0, 1)
                 dual = t_mass[a, self.rows] / sums
-                t_band[it, self.spot(a, p, q), self.rows] = dual.astype(BF16)
+                t_band[h][it, self.spot(a, p, q)] = dual.astype(BF16)
                 for kind in (2, 0, 1):
                     self.q_copy(a, kind).start()
                 t_all[a, self.rows] = dual
@@ -561,35 +577,38 @@
                 self.z_copy(1, r).wait_send()
 
     def iteration(it, _):
-        chains = [Chain(h, it) for h in range(CHAINS)]
+        first, second = chains = [Chain(h, it) for h in range(CHAINS)]
+
+        def both(*names):
+            for name in names:
+                for chain in chains:
+                    getattr(chain, name)()
+
+        for d in (2, 1, 3):
+            first.stage(d)
+        first.ring_first()
 
         @pl.when(it > 0)
         def _():
-            for h in range(CHAINS):
-                source_arrived(1, h)
-
-            @pl.loop(0, slots // GROUP)
-            def _(group):
-                for m in range(GROUP):
-                    row_product(1, group * GROUP + m)
-
-        for d in (2, 1, 3, 0):
-            for chain in chains:
-                chain.stage(d)
-        for name in ("ring_first", "ring_relay", "ring_sum", "ring_total",
-                     "target", "gather_near", "gather_block", "gather_relay",
-                     "gather_last"):
-            for chain in chains:
-                getattr(chain, name)()
-            if name == "ring_first":
-                @pl.when(it == 0)
-                def _():
-                    @pl.when(swapped)
-                    def _():
-                        tm_copy.wait_recv()
-
-                    for k in range(2):
-                        t_mass[k] = tm_in[k * tile:(k + 1) * tile, :].T
+            source_arrived(1, 1)
+            products(row_product, 1, 1)
+
+        for d in (2, 1, 3):
+            second.stage(d)
+        second.ring_first()
+        first.stage(0)
+        second.stage(0)
+
+        @pl.when(it == 0)
+        def _():
+            @pl.when(swapped)
+            def _():
+                tm_copy.wait_recv()
+
+            for k in range(2):
+                t_mass[k] = tm_in[k * tile:(k + 1) * tile, :].T
+
+        both("ring_relay", "ring_sum", "ring_total", "target", "gather_near", "gather_block")
 
         @pl.when(it == ITERS - 1)
         def _():
@@ -604,25 +623,30 @@
             def _():
                 td_out[...] = td_own[...]
 
-        for chain in chains:
-            chain.gathered()
-
-        @pl.loop(0, slots // GROUP)
-        def _(group):
-            for m in range(GROUP):
-                s = group * GROUP + m
-                acc[s] = acc[meta[3, s]] + lax.dot_general(
-                    t_band[it, meta[6, s]], kt[s], (((1,), (1,)), ((), ())),
-                    preferred_element_type=F32)
-
-        for name in ("to_owner", "to_owner_relay", "source"):
-            for chain in chains:
-                getattr(chain, name)()
+        both("gather_relay")
+        first.gather_last()
+        first.gathered()
+        products(column_product, it, 0)
+        first.to_owner()
+        second.gather_last()
+        second.gathered()
+        products(column_product, it, 1)
+        first.to_owner_relay()
+        second.to_owner()
+        first.source()
+        second.to_owner_relay()
 
         @pl.when(it < ITERS - 1)
         def _():
-            for h in range(CHAINS):
-                source_pass_on(1, h)
+            source_pass_on(1, 0)
+
+        second.source()
+
+        @pl.when(it < ITERS - 1)
+        def _():
+            source_arrived(1, 0)
+            products(row_product, 1, 0)
+            source_pass_on(1, 1)
 
         for chain in chains:
             chain.sent()
@@ -674,7 +698,7 @@
             vmem((slots, tile, tile), BF16),
             vmem((slots + 1, measures, tile), F32),
             vmem((ITERS, 2, measures, tile), BF16),
-            vmem((ITERS, 8, measures, tile), BF16),
+            [vmem((ITERS, 8, mh, tile), BF16)] * CHAINS,
             vmem((CHAINS, 4, 2, 4, mh, tile), F32),
             vmem((CHAINS, 4, 2, 4, mh, tile), F32),
             vmem((CHAINS, 2, 4, 4 * mh + 16, tile), I16),
@@ -682,7 +706,7 @@
             vmem((CHAINS, 2, 3, mh + 16, tile), I16),
             vmem((ITERS, CHAINS, 2, 3, mh + 16, tile), I16),
             vmem((CHAINS, 2, 4, mh, tile), F32),
-            vmem((ITERS, 64, measures, tile), BF16),
+            [vmem((ITERS, 64, mh, tile), BF16)] * CHAINS,
             vmem((CHAINS, 4, block, tile), I16),
             vmem((ITERS, CHAINS, 4, block, tile), I16),
             vmem((rows, measures), F32),

time: 133 us -> 138 us (1.038)
  Pallas kernels: 129 us -> 134 us
    pallas_call x1, Pallas kernels: 129 us -> 134 us  [local(): pl.pallas_call(functools.partial(kernel, slots), out_shape=(jax.ShapeDtyp...]
where the time goes in v10:
time: 138 us
  Pallas kernels  134 us (97%)
  local copies, waits for them, and re-layouts  2.42 us (2%)
    pallas_call x1, Pallas kernels, local(): pl.pallas_call(functools.partial(kernel, slots), out_shape=(jax.ShapeDtyp...  134 us

profile of v10, /device:TPU:1, one launch (start us, length us, event | category | flops | bytes accessed | tf_op | source)
XLA Modules:
  0.0 137.9 jit_solution(18249894631872694895)
XLA Ops:
  1.3 134.2 %shard_map.95 = (f32[512,128]{1,0:T(8,128)}, f32[512,128]{1,0:T(8,128)}) custom-call(f32[3,16384]{1,0:T(4,128)} %tp.1, f32[3,2048]{1,0:T(4,128)} %sp.1, f32[512,128]{1,0:T(8,128)} %tm.1, f32[512,128]{1,0:T(8,128)} %sm.1, bf16[512,128]{1,0:T(8,128)(2,1)} %sd.1, s32[1,48]{1,0:T(1,128)} %bitcast.2, s32[1,48]{1,0:T(1,128)} %bitcast.3, s32[1]{0:T(128)S(6)} %copy.12.tn), custom_call_target="tpu_custom_call" | custom-call | tf_op jit(solution)/shard_map/pallas_call | solution.py:681
  135.5 0.0 copy-start
  135.5 1.7 %copy.13 = f32[512,128]{1,0:T(8,128)} copy(f32[512,128]{1,0:T(8,128)} %get-tuple-element.4) | data formatting | bytes 524288
  137.2 0.0 copy-done
  137.2 0.7 copy.14
Async XLA Ops:
  135.5 1.7 %copy-start = (f32[512,128]{1,0:T(8,128)S(1)}, f32[512,128]{1,0:T(8,128)}, u32[]{:S(2)}) copy-start(f32[512,128]{1,0:T(8,128)} %get-tuple-element.5) | copy-start | bytes 786436

commit v11 on v9

--- a/solution.py
+++ b/solution.py
@@ -10,7 +10,7 @@
 MESH = pl.DeviceIdType.MESH
 ITERS = 2
 CHAINS = 2
-GROUP = 16
+GROUP = 24
 SCALE = 2.6857913
 FINE = 2896.0
 COARSE = 256.0
@@ -577,11 +577,15 @@
         for chain in chains:
             for d in (2, 1, 3):
                 chain.stage(d)
-        for name in ("ring_first", "ring_relay", "ring_sum", "ring_total",
-                     "target", "gather_near", "gather_block", "gather_relay",
-                     "gather_last"):
-            for chain in chains:
-                getattr(chain, name)()
+        order = [(name, h) for name in ("ring_first", "ring_relay") for h in range(CHAINS)]
+        order += [("ring_sum", 0), ("ring_total", 0), ("ring_sum", 1), ("ring_total", 1),
+                  ("target", 0), ("target", 1), ("gather_near", 0), ("gather_near", 1),
+                  ("gather_block", 0), ("gather_block", 1), ("gather_relay", 0),
+                  ("gather_relay", 1), ("gather_last", 0), ("gather_last", 1)]
+        for name, h in order:
+            getattr(chains[h], name)()
+            if h < CHAINS - 1:
+                continue
             if name == "gather_block":
                 @pl.when(it == ITERS - 1)
                 def _():

time: 132 us -> 131 us (level)
  no operation moved by 1% of the time
where the time goes in v11:
time: 131 us
  Pallas kernels  127 us (97%)
  local copies, waits for them, and re-layouts  2.42 us (2%)
    pallas_call x1, Pallas kernels, local(): pl.pallas_call(functools.partial(kernel, slots), out_shape=(jax.ShapeDtyp...  127 us

profile of v11, /device:TPU:1, one launch (start us, length us, event | category | flops | bytes accessed | tf_op | source)
XLA Modules:
  0.0 130.9 jit_solution(13434913181258857516)
XLA Ops:
  1.3 127.1 %shard_map.95 = (f32[512,128]{1,0:T(8,128)}, f32[512,128]{1,0:T(8,128)}) custom-call(f32[3,16384]{1,0:T(4,128)} %tp.1, f32[3,2048]{1,0:T(4,128)} %sp.1, f32[512,128]{1,0:T(8,128)} %tm.1, f32[512,128]{1,0:T(8,128)} %sm.1, bf16[512,128]{1,0:T(8,128)(2,1)} %sd.1, s32[1,48]{1,0:T(1,128)} %bitcast.2, s32[1,48]{1,0:T(1,128)} %bitcast.3, s32[1]{0:T(128)S(6)} %copy.12.tn), custom_call_target="tpu_custom_call" | custom-call | tf_op jit(solution)/shard_map/pallas_call | solution.py:666
  128.4 0.0 copy-start
  128.4 1.7 %copy.13 = f32[512,128]{1,0:T(8,128)} copy(f32[512,128]{1,0:T(8,128)} %get-tuple-element.4) | data formatting | bytes 524288
  130.2 0.0 copy-done
  130.2 0.7 copy.14
Async XLA Ops:
  128.4 1.7 %copy-start = (f32[512,128]{1,0:T(8,128)S(1)}, f32[512,128]{1,0:T(8,128)}, u32[]{:S(2)}) copy-start(f32[512,128]{1,0:T(8,128)} %get-tuple-element.5) | copy-start | bytes 786436
